TPU v7x, 32 devices: a whole 2x2x4 slice. The times are simulated.
32 devices in a mesh: parts: 2 (over y), tensor: 4 (over x, core), batch: 4 (over z).
Axes of the slice: x: 2, y: 2, z: 4, core: 2. Of those that a mesh axis runs over, the one named last changes fastest.
Arguments:
- frames: bfloat16 [640, 5120], P(('parts', 'batch'), 'tensor'), parts along dimension 0, may hold values from -6 to 6
- send_index: int32 [8, 4, 16], P('parts'), parts along dimension 0, may hold values from -1 to 79, as said below
- row_segment: int32 [640], P('parts'), parts along dimension 0, may hold values from -1 to 319, as said below
- attn_gain: float32 [5120], replicated, may hold values from 0.1 to 1.9
- q_weight: bfloat16 [5120, 4096], P('batch', 'tensor'), may hold values from -0.078125 to 0.078125
- kv_weight: bfloat16 [5120, 2048], P('batch'), may hold values from -0.078125 to 0.078125
- out_weight: bfloat16 [4096, 5120], P(('tensor', 'batch')), may hold values from -0.09375 to 0.09375
- ffn_gain: float32 [5120], replicated, may hold values from 0.1 to 1.9
- gate_weight: bfloat16 [5120, 32768], P(None, ('tensor', 'batch')), may hold values from -0.078125 to 0.078125
- up_weight: bfloat16 [5120, 32768], P(None, ('tensor', 'batch')), may hold values from -0.078125 to 0.078125
- down_weight: bfloat16 [32768, 5120], P('tensor', 'batch'), may hold values from -0.03125 to 0.03125
Outputs:
- mixed: bfloat16 [512, 5120], P(('parts', 'tensor'), 'batch'), parts along dimension 0
There are 2 independent parts, one for each index of `parts`. A program takes and returns all parts, laid end to end along the dimension named above; an argument that names none is the same for every part. Nothing has to cross between parts.
Inputs may be any that keep to these rules, and one draw needn't show every extreme that they name: `send_index`: entry [s, g, c] is a row of owner s; for each s and g the live entries come first and are consecutive rising rows, then -1. For one owner, the rows sent to different groups are distinct. Each group receives at most 16 rows from one owner, and in every draw one group receives 16 rows from every owner. `row_segment`: live rows that one owner sends to one group and that share an id are consecutive and form a segment; ids differ between owners and between the groups one owner sends to.
All inputs are finite; a program needn't handle non-finite values.
Results may differ from a plain program's by a relative error of at most 0.0076.
Values may be sent and summed in bfloat16 or wider, within the bound.
No kernel may reach another device: no remote copies, remote signals or barrier semaphores. Data moves between devices by JAX's collectives and lax.ppermute only.
A program may use at most 192 MiB of HBM per device.

v0:
```python
import math

import jax
import jax.numpy as jnp
from jax import lax
from jax.sharding import PartitionSpec as P

HEADS = 32
KV_HEADS = 8
HEAD_DIM = 128


EPSILON = 1e-05
ROPE_BASE = 1000000000.0


def rms_rows(values, gain):
    wide = values.astype(jnp.float32)
    factor = lax.rsqrt(jnp.mean(wide * wide, axis=-1, keepdims=True) + EPSILON)
    return (wide * factor * gain).astype(jnp.bfloat16)


def rotate(values, positions):
    head_dim = values.shape[-1]
    half = head_dim // 2
    freq = jnp.exp(jnp.arange(half).astype(jnp.float32) * (-2.0 * math.log(ROPE_BASE) / head_dim))
    angle = positions.astype(jnp.float32)[:, None] * freq[None, :]
    cosine = jnp.cos(angle)[:, None, :]
    sine = jnp.sin(angle)[:, None, :]
    first = values[..., :half]
    second = values[..., half:]
    return jnp.concatenate(
        [first * cosine - second * sine, second * cosine + first * sine], axis=-1
    )


def segment_mask(ids):
    order = jnp.arange(ids.shape[0], dtype=jnp.int32)
    allowed = (ids[:, None] == ids[None, :]) & (order[None, :] <= order[:, None])
    positions = jnp.sum(allowed.astype(jnp.int32), axis=1) - 1
    return (allowed, positions)


def attend(queries, keys, values, allowed):
    count, heads, head_dim = queries.shape
    kv_heads = keys.shape[1]
    grouped = queries.reshape(count, kv_heads, heads // kv_heads, head_dim)
    scores = jnp.einsum(
        "qkgd,skd->kgqs", grouped, keys, preferred_element_type=jnp.float32
    ) / math.sqrt(head_dim)
    scores = jnp.where(allowed[None, None], scores, -1e30)
    top = jnp.max(scores, axis=-1, keepdims=True)
    weights = jnp.exp(scores - top)
    probs = (weights / jnp.sum(weights, axis=-1, keepdims=True)).astype(jnp.bfloat16)
    context = jnp.einsum("kgqs,skd->qkgd", probs, values, preferred_element_type=jnp.float32)
    return context.reshape(count, heads * head_dim).astype(jnp.bfloat16)


def per_device(
    frames,
    send_index,
    row_segment,
    attn_gain,
    q_weight,
    kv_weight,
    out_weight,
    ffn_gain,
    gate_weight,
    up_weight,
    down_weight,
):
    groups = lax.axis_size("batch")
    tensors = lax.axis_size("tensor")
    group_index = lax.axis_index("batch")
    tensor_index = lax.axis_index("tensor")
    owned = frames.shape[0]
    capacity = send_index.shape[2]
    slot_count = groups * capacity
    outgoing = lax.dynamic_index_in_dim(send_index, group_index, 0, keepdims=False).reshape(
        slot_count
    )
    picked = jnp.take(frames, jnp.maximum(outgoing, 0), axis=0)
    picked = jnp.where((outgoing >= 0)[:, None], picked, jnp.zeros_like(picked))
    arrived = lax.all_to_all(picked, "batch", split_axis=0, concat_axis=0, tiled=True)
    incoming = lax.dynamic_index_in_dim(send_index, group_index, 1, keepdims=False)
    sources = jnp.arange(groups, dtype=jnp.int32)[:, None] * owned
    looked = jnp.take(row_segment, (sources + jnp.maximum(incoming, 0)).reshape(slot_count))
    segment_ids = jnp.where(incoming.reshape(slot_count) >= 0, looked, -1)
    allowed, positions = segment_mask(segment_ids)
    rows = lax.all_gather(arrived, "tensor", axis=1, tiled=True)
    normed = rms_rows(rows, attn_gain)
    local_heads = q_weight.shape[1] // HEAD_DIM
    share_group = HEADS // KV_HEADS
    local_kv = max(1, local_heads // share_group)
    first_kv = tensor_index * local_heads // share_group
    kv_columns = lax.dynamic_slice_in_dim(
        kv_weight, first_kv * (2 * HEAD_DIM), local_kv * 2 * HEAD_DIM, 1
    )
    section = normed
    query_all = jnp.dot(
        section,
        lax.all_gather(q_weight, "batch", axis=0, tiled=True),
        preferred_element_type=jnp.float32,
    )
    pair_all = jnp.dot(
        section,
        lax.all_gather(kv_columns, "batch", axis=0, tiled=True),
        preferred_element_type=jnp.float32,
    )
    queries = rotate(query_all.reshape(slot_count, local_heads, HEAD_DIM), positions).astype(
        jnp.bfloat16
    )
    pairs = pair_all.reshape(slot_count, local_kv, 2, HEAD_DIM)
    keys = rotate(pairs[:, :, 0], positions).astype(jnp.bfloat16)
    values = pairs[:, :, 1].astype(jnp.bfloat16)
    context = attend(queries, keys, values, allowed)
    section = context
    partial_out = jnp.dot(
        section,
        lax.all_gather(out_weight, "batch", axis=0, tiled=True),
        preferred_element_type=jnp.float32,
    )
    share = lax.psum_scatter(partial_out, "tensor", scatter_dimension=1, tiled=True)
    resid = (arrived.astype(jnp.float32) + share).astype(jnp.bfloat16)
    blocks = lax.all_gather(resid, "batch", axis=0, tiled=True)
    everything = lax.all_gather(blocks, "tensor", axis=1, tiled=True)
    normed2 = rms_rows(everything, ffn_gain)
    gate = jnp.dot(normed2, gate_weight, preferred_element_type=jnp.float32)
    upper = jnp.dot(normed2, up_weight, preferred_element_type=jnp.float32)
    hidden = (jax.nn.silu(gate) * upper).astype(jnp.bfloat16)
    projected = jnp.dot(
        lax.all_gather(hidden, "batch", axis=1, tiled=True),
        down_weight,
        preferred_element_type=jnp.float32,
    )
    reduced = lax.psum_scatter(projected, "tensor", scatter_dimension=0, tiled=True)
    rows_each = everything.shape[0] // tensors
    width_each = down_weight.shape[1]
    residual_block = lax.dynamic_slice(
        everything, (tensor_index * rows_each, group_index * width_each), (rows_each, width_each)
    )
    return (residual_block.astype(jnp.float32) + reduced).astype(jnp.bfloat16)


def solution(mesh):
    in_specs = (
        P(("parts", "batch"), "tensor"),
        P("parts", None, None),
        P("parts"),
        P(),
        P("batch", "tensor"),
        P("batch", None),
        P(("tensor", "batch"), None),
        P(),
        P(None, ("tensor", "batch")),
        P(None, ("tensor", "batch")),
        P("tensor", "batch"),
    )
    out_specs = P(("parts", "tensor"), "batch")
    return jax.shard_map(
        per_device, mesh=mesh, in_specs=in_specs, out_specs=out_specs, check_vma=False
    )
```

profile of v0, /device:TPU:0, one launch (start us, length us, event | category | flops | bytes accessed | tf_op | source)
XLA Modules:
  0.0 708.9 jit_solution(356064087127464896)
XLA Ops:
  6.5 0.0 copy-start
  6.5 0.0 all-gather.6.cloned.1.call-start
  6.5 2.5 constant_dynamic-slice_fusion
  9.1 0.0 all-gather.6.cloned.1.call-update
  9.1 0.0 copy-start.4
  9.1 0.0 all-gather.8.cloned.1.call-start
  9.2 0.7 all-gather.8.cloned.1.call-update
  9.9 0.0 all-gather.10.cloned.1.call-start
  9.9 0.7 all-gather.10.cloned.1.call-update
  10.6 0.0 copy-done.5
  10.6 0.1 reshape.275
  10.7 0.0 copy-done
  10.7 0.7 gather_fusion
  11.4 0.8 select_select_fusion
  12.2 6.3 all-to-all-start
  18.5 0.0 reduce-scatter.3.cloned.1.call-start
  18.5 0.1 add.132
  18.6 0.1 add.137
  18.7 0.1 add.133
  18.8 0.6 broadcast.278
  19.3 0.6 fusion.51
  20.0 0.1 max.48
  20.1 0.1 max.47
  20.2 0.1 ge.51
  20.3 0.8 gather_fusion.1
  21.1 0.1 convert_reduce_fusion
  21.2 0.1 fusion.26
  21.3 0.2 multiply_cosine_fusion
  21.5 3.5 all-to-all-done
  25.0 7.9 %all_gather.21 = bf16[64,5120]{1,0:T(8,128)(2,1)S(1)} all-gather(bf16[64,1280]{1,0:T(8,128)(2,1)S(1)} %bitcast.64), channel_id=1, replica_groups=mesh['parts'=2,'tensor'=4,'batch'=4] {'tensor'}, dimensions={1}, use_global_device_ids=true | all-gather | bytes 819200 | tf_op jit(solution)/shard_map/all_gather | solution.py:90
  32.9 0.2 fusion.5
  33.2 77.3 %all-gather.6.cloned.1.call-done = bf16[5120,512]{1,0:T(8,128)(2,1)} async-done(((bf16[1280,512]{1,0:T(8,128)(2,1)}), bf16[5120,512]{1,0:T(8,128)(2,1)}) %all-gather.6.cloned.1.call-update) | async-done | bytes 5242896 | tf_op jit(solution)/shard_map/all_gather | solution.py:107
  110.5 3.6 fusion.17
  114.0 0.1 reshape.271
  114.2 0.1 slice.29
  114.3 0.1 subtract_convert_fusion.1
  114.4 180.6 %all-gather.8.cloned.1.call-done = bf16[5120,1024]{1,0:T(8,128)(2,1)} async-done(((bf16[1280,1024]{1,0:T(8,128)(2,1)}), bf16[5120,1024]{1,0:T(8,128)(2,1)}) %all-gather.8.cloned.1.call-update) | async-done | bytes 10485776 | tf_op jit(solution)/shard_map/all_gather | solution.py:102
  295.0 6.0 convolution_bitcast_fusion
  301.0 0.2 subtract_convert_fusion
  301.3 0.4 fusion.52
  301.6 0.6 fusion.12
  302.2 0.1 copy.22
  302.3 0.1 convert_element_type.75
  302.4 176.3 %all-gather.10.cloned.1.call-done = bf16[1024,5120]{1,0:T(8,128)(2,1)} async-done(((bf16[256,5120]{1,0:T(8,128)(2,1)}), bf16[1024,5120]{1,0:T(8,128)(2,1)}) %all-gather.10.cloned.1.call-update) | async-done | bytes 10485776 | tf_op jit(solution)/shard_map/all_gather | solution.py:120
  478.7 7.0 fusion.55
  485.7 0.0 reduce-scatter.3.cloned.1.call-update
  485.7 0.0 all-gather.12.cloned.1.call-start
  485.8 24.8 %reduce-scatter.3.cloned.1.call-done = f32[64,1280]{1,0:T(8,128)} async-done(((f32[64,5120]{1,0:T(8,128)}), f32[64,1280]{1,0:T(8,128)}) %reduce-scatter.3.cloned.1.call-update) | async-done | bytes 327696 | tf_op jit(solution)/shard_map/reduce_scatter | solution.py:123
  510.6 1.0 add_convert_fusion.1
  511.6 17.7 %all_gather.25 = bf16[256,1280]{1,0:T(8,128)(2,1)} all-gather(bf16[64,1280]{1,0:T(8,128)(2,1)S(1)} %add_convert_fusion.1), channel_id=1, replica_groups=mesh['parts'=2,'tensor'=4,'batch'=4] {'batch'}, dimensions={0}, use_global_device_ids=true | all-gather | bytes 819200 | tf_op jit(solution)/shard_map/all_gather | solution.py:125
  529.3 0.0 all-gather.12.cloned.1.call-update
  529.3 0.2 all-gather.14.cloned.1.call-start
  529.6 25.7 %all-gather.12.cloned.1.call-done = bf16[256,5120]{1,0:T(8,128)(2,1)} async-done(((bf16[256,1280]{1,0:T(8,128)(2,1)}), bf16[256,5120]{1,0:T(8,128)(2,1)}) %all-gather.12.cloned.1.call-update) | async-done | bytes 2621456 | tf_op jit(solution)/shard_map/all_gather | solution.py:126
  555.3 2.3 fusion.1
  557.7 10.8 %fusion.14 = f32[256,2048]{1,0:T(8,128)S(1)} fusion(bf16[5120,2048]{1,0:T(8,128)(2,1)} %param.19, bf16[256,5120]{1,0:T(8,128)(2,1)} %all-gather.12.cloned.1.call-done, f32[5120]{0:T(1024)S(1)} %copy-done.6, f32[256]{0:T(256)S(1)} %add_rsqrt_fusion), kind=kOutput, calls=%fused_computation.23 | convolution fusion | flops 5373952000 | bytes 25711616 | tf_op jit(solution)/shard_map/dot_general | solution.py:128
  568.5 0.0 copy-done.3
  568.5 11.5 %fusion.4 = bf16[256,2048]{1,0:T(8,128)(2,1)} fusion(bf16[5120,2048]{1,0:T(8,128)(2,1)} %param.20, f32[256,2048]{1,0:T(8,128)S(1)} %fusion.14, bf16[256,5120]{1,0:T(8,128)(2,1)S(1)} %copy-done.3, f32[5120]{0:T(1024)S(1)} %copy-done.6, f32[256]{0:T(256)S(1)} %add_rsqrt_fusion), kind=kOutput, calls=%fused_computation.9 | convolution fusion | flops 5377097728 | bytes 26760192 | tf_op jit(solution)/shard_map/dot_general | solution.py:129
  580.0 0.0 all-gather.14.cloned.1.call-update
  580.0 0.0 reduce-scatter.5.cloned.1.call-start
  580.0 80.9 %all-gather.14.cloned.1.call-done = bf16[256,8192]{1,0:T(8,128)(2,1)} async-done(((bf16[256,2048]{1,0:T(8,128)(2,1)}), bf16[256,8192]{1,0:T(8,128)(2,1)}) %all-gather.14.cloned.1.call-update) | async-done | bytes 4194320 | tf_op jit(solution)/shard_map/all_gather | solution.py:132
  660.9 14.2 %fusion.56 = f32[256,1280]{1,0:T(8,128)} fusion(bf16[256,8192]{1,0:T(8,128)(2,1)} %all-gather.14.cloned.1.call-done, bf16[8192,1280]{1,0:T(8,128)(2,1)} %param.21), kind=kOutput, calls=%fused_computation.77 | convolution fusion | flops 5368709120 | bytes 26476544 | tf_op jit(solution)/shard_map/dot_general | solution.py:131
  675.2 0.0 reduce-scatter.5.cloned.1.call-update
  675.2 25.2 %reduce-scatter.5.cloned.1.call-done = f32[64,1280]{1,0:T(8,128)} async-done(((f32[256,1280]{1,0:T(8,128)}), f32[64,1280]{1,0:T(8,128)}) %reduce-scatter.5.cloned.1.call-update) | async-done | bytes 327696 | tf_op jit(solution)/shard_map/reduce_scatter | solution.py:136
  700.4 1.7 add_convert_fusion
  (25 shorter events, 0.3 us)
Async XLA Ops:
  6.5 4.2 copy-start
  6.5 103.9 %all-gather.6.cloned.1.call-start = ((), (), s32[]{:S(2)}) async-start(), calls=%async_computation.3 | async-start | bytes 6553600 | tf_op jit(solution)/shard_map/all_gather | solution.py:107
  6.5 4.1 copy-start.5
  9.1 11.2 %copy-start.2 = (s32[320]{0:T(512)S(1)}, s32[320]{0:T(512)}, u32[]{:S(2)}) copy-start(s32[320]{0:T(512)} %param.13) | copy-start | bytes 3844
  9.1 101.4 %copy-start.4 = (f32[5120]{0:T(1024)S(1)}, f32[5120]{0:T(1024)}, u32[]{:S(2)}) copy-start(f32[5120]{0:T(1024)} %param.14) | copy-start | bytes 61444
  9.1 285.9 %all-gather.8.cloned.1.call-start = ((), (), s32[]{:S(2)}) async-start(), calls=%async_computation.4 | async-start | bytes 13107200 | tf_op jit(solution)/shard_map/all_gather | solution.py:102
  9.9 468.9 %all-gather.10.cloned.1.call-start = ((), (), s32[]{:S(2)}) async-start(), calls=%async_computation.5 | async-start | bytes 13107200 | tf_op jit(solution)/shard_map/all_gather | solution.py:120
  12.2 12.8 %all-to-all-start = ((bf16[4,16,1280]{2,1,0:T(8,128)(2,1)}), bf16[4,16,1280]{2,1,0:T(8,128)(2,1)S(1)}, u32[]{:S(2)}, u32[]{:S(2)}) async-start(bf16[4,16,1280]{2,1,0:T(8,128)(2,1)} %select_select_fusion), calls=%async_computation | async-start | bytes 327680 | tf_op jit(solution)/shard_map/all_to_all | solution.py:84
  18.5 492.1 %reduce-scatter.3.cloned.1.call-start = ((), (), s32[]{:S(2)}) async-start(), calls=%async_computation.6 | async-start | bytes 1638400 | tf_op jit(solution)/shard_map/reduce_scatter | solution.py:123
  485.7 72.0 %copy-start.6 = (f32[5120]{0:T(1024)S(1)}, f32[5120]{0:T(1024)}, u32[]{:S(2)}) copy-start(f32[5120]{0:T(1024)} %param.18) | copy-start | bytes 61444
  485.7 69.6 %all-gather.12.cloned.1.call-start = ((), (), s32[]{:S(2)}) async-start(), calls=%async_computation.7 | async-start | bytes 3276800 | tf_op jit(solution)/shard_map/all_gather | solution.py:126
  529.3 131.6 %all-gather.14.cloned.1.call-start = ((), (), s32[]{:S(2)}) async-start(), calls=%async_computation.8 | async-start | bytes 5242880 | tf_op jit(solution)/shard_map/all_gather | solution.py:132
  557.7 10.8 %copy-start.3 = (bf16[256,5120]{1,0:T(8,128)(2,1)S(1)}, bf16[256,5120]{1,0:T(8,128)(2,1)}, u32[]{:S(2)}) copy-start(bf16[256,5120]{1,0:T(8,128)(2,1)} %all-gather.12.cloned.1.call-done) | copy-start | bytes 7864324
  580.0 120.4 %reduce-scatter.5.cloned.1.call-start = ((), (), s32[]{:S(2)}) async-start(), calls=%async_computation.9 | async-start | bytes 1638400 | tf_op jit(solution)/shard_map/reduce_scatter | solution.py:136
  660.9 41.2 %copy-start.1 = (bf16[80,1280]{1,0:T(8,128)(2,1)S(1)}, bf16[80,1280]{1,0:T(8,128)(2,1)}, u32[]{:S(2)}) copy-start(bf16[80,1280]{1,0:T(8,128)(2,1)} %param.11) | copy-start | bytes 614404
Sparse Core Ops, SparseCore 0:
  9.2 101.2 all-gather.5
  112.0 182.9 all-gather.7
  296.6 182.0 all-gather.9
  485.8 24.7 reduce-scatter.2
  529.5 25.7 all-gather.11
  580.1 80.7 all-gather.13
  675.3 25.0 reduce-scatter.4
where the time goes:
time: 709 us
  waiting for transfers between devices  596 us (84%)
  matrix products  54 us (8%)
  blocking collectives  25.6 us (4%)
  between operations  13.7 us (2%)
  other arithmetic  7.4 us (1%)
    all_gather x1, waiting for transfers between devices, per_device(): lax.all_gather(q_weight, 'batch', axis=0, tiled=True)  181 us
    all_gather x1, waiting for transfers between devices, per_device(): lax.all_gather(out_weight, 'batch', axis=0, tiled=True)  176 us
    all_gather x1, waiting for transfers between devices, per_device(): lax.all_gather(hidden, 'batch', axis=1, tiled=True)  80.9 us
    all_gather x1, waiting for transfers between devices, per_device(): lax.all_gather(kv_columns, 'batch', axis=0, tiled=True)  77.3 us
    all_gather x1, waiting for transfers between devices, per_device(): everything = lax.all_gather(blocks, 'tensor', axis=1, tiled=True)  25.7 us
    reduce_scatter x1, waiting for transfers between devices, per_device(): lax.psum_scatter(projected, 'tensor', scatter_dimension=0, tiled=True)  25.2 us
    reduce_scatter x1, waiting for transfers between devices, per_device(): lax.psum_scatter(partial_out, 'tensor', scatter_dimension=1, tiled=True)  24.8 us
    all_gather x1, blocking collectives, per_device(): blocks = lax.all_gather(resid, 'batch', axis=0, tiled=True)  17.7 us
  transfers between devices with their start and end apart: 8, of which 8 were waited for; matrix products, arithmetic and copies ran while one was open for 2% of the time, Pallas kernels for 0%

commit v1 on v0

--- a/solution.py
+++ b/solution.py
@@ -1,8 +1,11 @@
+import functools
 import math
 
 import jax
 import jax.numpy as jnp
 from jax import lax
+from jax.experimental import pallas as pl
+from jax.experimental.pallas import tpu as pltpu
 from jax.sharding import PartitionSpec as P
 
 HEADS = 32
@@ -142,6 +145,394 @@
     return (residual_block.astype(jnp.float32) + reduced).astype(jnp.bfloat16)
 
 
+CORE_SWAP = [(0, 1), (1, 0), (2, 3), (3, 2)]
+CHIP_SWAP = [(0, 2), (2, 0), (1, 3), (3, 1)]
+PAIRS_OUTER = [(0, 1), (1, 0), (2, 3), (3, 2)]
+PAIRS_INNER = [(0, 0), (1, 2), (2, 1), (3, 3)]
+CHUNKS = 4
+F32 = jnp.float32
+BF16 = jnp.bfloat16
+
+
+def dot(a, b):
+    return jnp.dot(a, b, preferred_element_type=F32)
+
+
+def shift(values, distance):
+    return lax.ppermute(values, "batch", [(i, (i + distance) % 4) for i in range(4)])
+
+
+def call(body, name, out_shape, operands, scalars, grid=(1,), in_specs=None, out_specs=None,
+         scratch=(), aliases=None, flops=0, moved=0, limit=40):
+    whole = lambda a: pl.BlockSpec(a.shape, lambda *_, n=len(a.shape): (0,) * n)
+    if in_specs is None:
+        in_specs = [None] * len(operands)
+    in_specs = [whole(a) if s is None else s for s, a in zip(in_specs, operands)]
+    if out_specs is None:
+        out_specs = jax.tree.map(whole, out_shape)
+    return pl.pallas_call(
+        body,
+        out_shape=out_shape,
+        grid_spec=pltpu.PrefetchScalarGridSpec(
+            num_scalar_prefetch=1, grid=grid, in_specs=in_specs, out_specs=out_specs,
+            scratch_shapes=list(scratch),
+        ),
+        compiler_params=pltpu.CompilerParams(vmem_limit_bytes=limit << 20),
+        input_output_aliases=aliases or {},
+        cost_estimate=pl.CostEstimate(flops=int(flops), bytes_accessed=int(moved), transcendentals=0),
+        name=name,
+    )(scalars, *operands)
+
+
+def norm_send_body(where, own, core, chip, both, gain, out):
+    t, b = where[0], where[1]
+    wide = [ref[...].astype(F32) for ref in (own, core, chip, both)]
+    total = sum(jnp.sum(w * w, axis=-1, keepdims=True) for w in wide)
+    factor = lax.rsqrt(total / (4 * own.shape[1]) + EPSILON)
+    for j in range(4):
+        block = lax.bitwise_xor(t, j)
+        d = lax.rem(block - b + 4, 4)
+        out[d] = (wide[j] * factor * gain[pl.ds(block, 1), :]).astype(BF16)
+
+
+def qkv_body(where, own, first, second, third, ranks, q_weight, kv_weight, kept, sent):
+    b = where[1]
+    rows = kept.shape[0]
+    spread = jnp.concatenate([own[0], first[...], second[...], third[...]], axis=0)
+    order = lax.broadcasted_iota(jnp.int32, (rows, ranks.shape[1]), 0)
+    pick = (order == ranks[...]).astype(F32).astype(BF16)
+    packed = dot(pick, spread).astype(BF16)
+    width = q_weight.shape[1] // 4
+    for k in range(4):
+        if k % 2 == 0:
+            pair = dot(packed, kv_weight[:, (k // 2) * 256:(k // 2 + 1) * 256])
+        query = dot(packed, q_weight[:, k * width:(k + 1) * width])
+        d = lax.rem(k - b + 4, 4)
+
+        @pl.when(d == 0)
+        def _():
+            kept[:, :width] = query
+            kept[:, width:] = pair
+
+        @pl.when(d > 0)
+        def _():
+            sent[d - 1, :, :width] = query.astype(BF16)
+            sent[d - 1, :, width:] = pair.astype(BF16)
+
+
+def attend_body(where, kept, first, second, third, cosine, sine, id_row, id_col, weight, sent, held):
+    t = where[0]
+    rows = kept.shape[0]
+    total = (kept[...] + first[...].astype(F32)) + (second[...].astype(F32) + third[...].astype(F32))
+    turn = lambda v: (v * cosine[...] + jnp.concatenate([v[:, 64:], v[:, :64]], axis=1) * sine[...]).astype(BF16)
+    key = turn(total[:, 256:384])
+    value = total[:, 384:].astype(BF16)
+    row = lax.broadcasted_iota(jnp.int32, (rows, rows), 0)
+    column = lax.broadcasted_iota(jnp.int32, (rows, rows), 1)
+    allowed = (id_col[...] == id_row[...]) & (column <= row)
+    parts = []
+    for h in range(2):
+        query = turn(total[:, h * 128:(h + 1) * 128])
+        scores = lax.dot_general(query, key, (((1,), (1,)), ((), ())), preferred_element_type=F32)
+        scores = jnp.where(allowed, scores / math.sqrt(HEAD_DIM), -1e30)
+        weights = jnp.exp(scores - jnp.max(scores, axis=-1, keepdims=True))
+        probs = (weights / jnp.sum(weights, axis=-1, keepdims=True)).astype(BF16)
+        parts.append(dot(probs, value).astype(BF16))
+    context = jnp.concatenate(parts, axis=1)
+    width = held.shape[2]
+    for j in (3, 1, 2, 0):
+        start = pl.multiple_of(lax.bitwise_xor(t, j) * width, 128)
+        product = dot(context, weight[:, pl.ds(start, width)])
+        if j % 2:
+            sent[j // 2] = product.astype(BF16)
+        else:
+            held[j // 2] = product
+
+
+def gather_sum_body(where, held, core, chip, raw, ranks, kept, sent):
+    b = where[1]
+    rows = held.shape[1]
+    order = lax.broadcasted_iota(jnp.int32, (rows, ranks.shape[1]), 0)
+    pick = (order == ranks[...]).astype(F32).astype(BF16)
+    total = held[0] + core[0].astype(F32) + chip[...].astype(F32) + dot(pick, raw[...])
+    each = rows // 4
+    for k in range(4):
+        piece = total[k * each:(k + 1) * each]
+        d = lax.rem(k - b + 4, 4)
+
+        @pl.when(d == 0)
+        def _():
+            kept[...] = piece
+
+        @pl.when(d > 0)
+        def _():
+            sent[d - 1] = piece.astype(BF16)
+
+
+def norm_all_body(where, own, chip, core, gain, out, resid):
+    t, b = where[0], where[1]
+    for d in range(4):
+        source = lax.rem(b - d + 4, 4)
+        wide = [ref.astype(F32) for ref in (own[d], core[0, d], chip[d], core[1, d])]
+        total = sum(jnp.sum(w * w, axis=-1, keepdims=True) for w in wide)
+        factor = lax.rsqrt(total / (4 * own.shape[2]) + EPSILON)
+        for j in range(4):
+            block = lax.bitwise_xor(t, j)
+            out[block, source] = (wide[j] * factor * gain[pl.ds(block, 1), :]).astype(BF16)
+
+            @pl.when(block == b)
+            def _():
+                resid[source] = wide[j].astype(BF16)
+
+
+def hidden_body(where, x, gate_weight, up_weight, out, gate, up):
+    k = pl.program_id(0)
+
+    @pl.when(k == 0)
+    def _():
+        gate[...] = dot(x[0], gate_weight[...])
+        up[...] = dot(x[0], up_weight[...])
+
+    @pl.when(k > 0)
+    def _():
+        gate[...] += dot(x[0], gate_weight[...])
+        up[...] += dot(x[0], up_weight[...])
+
+    @pl.when(k == pl.num_programs(0) - 1)
+    def _():
+        out[...] = (jax.nn.silu(gate[...]) * up[...]).astype(BF16)
+
+
+def hidden_chunk(where, x, gate_weight, up_weight, c):
+    blocks, rows, deep = x.shape
+    wide = gate_weight.shape[1] // CHUNKS
+    return call(
+        hidden_body, "hidden", jax.ShapeDtypeStruct((rows, wide), BF16), (x, gate_weight, up_weight), where,
+        grid=(blocks,),
+        in_specs=[
+            pl.BlockSpec((1, rows, deep), lambda k, w: (k, 0, 0)),
+            pl.BlockSpec((deep, wide), lambda k, w: (k, c)),
+            pl.BlockSpec((deep, wide), lambda k, w: (k, c)),
+        ],
+        scratch=[pltpu.VMEM((rows, wide), F32)] * 2,
+        flops=4 * rows * blocks * deep * wide, moved=4 * blocks * deep * wide,
+    )
+
+
+def down_products(where, refs, count):
+    inner = (where[1] == 1) | (where[1] == 2)
+    total = None
+    at = 0
+    for kind in count:
+        piece = refs[at][...]
+        at += 1
+        if kind == "either":
+            piece = jnp.where(inner, piece, refs[at][...])
+            at += 1
+        product = dot(piece, refs[at][...])
+        at += 1
+        total = product if total is None else total + product
+    return total
+
+
+def down_body(kinds, more, where, *refs):
+    total = down_products(where, refs[1:] if more else refs, kinds)
+    refs[-1][...] = total + refs[0][...] if more else total
+
+
+def down_last_body(kinds, where, acc, resid, slots, *refs):
+    t = where[0]
+    total = acc[...] + down_products(where, refs, kinds)
+    rounded = total.astype(BF16)
+    sent, held = refs[-2:]
+    rows = acc.shape[0]
+    order = lax.broadcasted_iota(jnp.int32, (slots.shape[1], rows), 1)
+    for j in range(4):
+        pick = (order == slots[lax.bitwise_xor(t, j)]).astype(F32).astype(BF16)
+        block = dot(pick, rounded)
+        if j == 0:
+            block = block + dot(pick, resid[...])
+        if j % 2:
+            sent[j // 2] = block.astype(BF16)
+        else:
+            held[j // 2] = block
+
+
+def down_operands(pieces, weight, tile):
+    operands, specs, kinds = [], [], []
+    for kind, arrays, position, c in pieces:
+        kinds.append(kind)
+        for a in arrays:
+            operands.append(a)
+            specs.append(pl.BlockSpec(a.shape, lambda n, w: (0, 0)))
+        operands.append(weight)
+        specs.append(
+            pl.BlockSpec((arrays[0].shape[1], tile), lambda n, w, p=position, c=c: (w[p] * CHUNKS + c, n))
+        )
+    return tuple(kinds), operands, specs
+
+
+def down(where, acc, pieces, weight, tile=256):
+    rows = pieces[0][1][0].shape[0]
+    width = weight.shape[1]
+    kinds, operands, specs = down_operands(pieces, weight, tile)
+    block = pl.BlockSpec((rows, tile), lambda n, w: (0, n))
+    more = acc is not None
+    deep = sum(a[0].shape[1] for _, a, _, _ in pieces)
+    return call(
+        functools.partial(down_body, kinds, more), "down", jax.ShapeDtypeStruct((rows, width), F32),
+        ([acc] if more else []) + operands, where, grid=(width // tile,),
+        in_specs=([block] if more else []) + specs, out_specs=block,
+        aliases={1: 0} if more else None, flops=2 * rows * deep * width, moved=2 * deep * width,
+    )
+
+
+def down_last(where, acc, resid, slots, pieces, weight, tile=256):
+    rows = acc.shape[0]
+    width = weight.shape[1]
+    count = slots.shape[1]
+    kinds, operands, specs = down_operands(pieces, weight, tile)
+    block = pl.BlockSpec((rows, tile), lambda n, w: (0, n))
+    deep = sum(a[0].shape[1] for _, a, _, _ in pieces)
+    out = pl.BlockSpec((2, count, tile), lambda n, w: (0, 0, n))
+    return call(
+        functools.partial(down_last_body, kinds), "down_last",
+        (jax.ShapeDtypeStruct((2, count, width), BF16), jax.ShapeDtypeStruct((2, count, width), F32)),
+        [acc, resid, slots] + operands, where, grid=(width // tile,),
+        in_specs=[block, block, None] + specs, out_specs=(out, out),
+        flops=2 * rows * deep * width, moved=2 * deep * width,
+    )
+
+
+def packed_layer(rows, where, picked, recv, ranks, own_ranks, slots, keys, gains, weights):
+    attn_kept, first, second, third = recv
+    q_weight, kv_weight, out_weight, gate_weight, up_weight, down_weight = weights
+    feature = picked.shape[1]
+    each = rows // 4
+    shape = jax.ShapeDtypeStruct
+
+    place = jnp.arange(rows, dtype=jnp.int32)
+    ids = jnp.sum(jnp.where(place[:, None] == ranks, keys + 1, 0), axis=1) - 1
+    allowed = (ids[:, None] == ids[None, :]) & (place[None, :] <= place[:, None])
+    positions = (jnp.sum(allowed.astype(jnp.int32), axis=1) - 1).astype(F32)
+    half = HEAD_DIM // 2
+    freq = jnp.exp(jnp.arange(half).astype(F32) * (-2.0 * math.log(ROPE_BASE) / HEAD_DIM))
+    angle = positions[:, None] * freq[None, :]
+    cosine, sine = jnp.cos(angle), jnp.sin(angle)
+    cosine = jnp.concatenate([cosine, cosine], axis=1)
+    sine = jnp.concatenate([-sine, sine], axis=1)
+
+    width = q_weight.shape[1] // 4 + 256
+    kept, sent = call(
+        qkv_body, "qkv", (shape((rows, width), F32), shape((3, rows, width), BF16)),
+        (attn_kept, first, second, third, ranks, q_weight, kv_weight), where,
+        in_specs=[pl.BlockSpec((1,) + attn_kept.shape[1:], lambda i, w: (0, 0, 0))] + [None] * 5
+        + [pl.BlockSpec((feature, 512), lambda i, w: (0, w[0]))],
+        flops=2 * rows * feature * 1536, moved=feature * 3072 + rows * 6000,
+    )
+    sums = [shift(sent[d - 1], d) for d in (1, 2, 3)]
+    sent, held = call(
+        attend_body, "attend", (shape((2, rows, feature), BF16), shape((2, rows, feature), F32)),
+        (kept, *sums, cosine, sine, ids[None, :], ids[:, None], out_weight), where,
+        flops=2 * rows * 256 * 5120, moved=256 * 10240 + rows * 30000,
+    )
+    core = lax.ppermute(sent, "tensor", CORE_SWAP)
+    chip = lax.ppermute((held[1] + core[1].astype(F32)).astype(BF16), "tensor", CHIP_SWAP)
+    kept, sent = call(
+        gather_sum_body, "gather_sum", (shape((each, feature), F32), shape((3, each, feature), BF16)),
+        (held, core, chip, picked, own_ranks), where,
+        in_specs=[pl.BlockSpec((1, rows, feature), lambda i, w: (0, 0, 0))] * 2 + [None] * 3,
+        flops=2 * rows * 64 * feature, moved=rows * feature * 10,
+    )
+    sums = [shift(sent[d - 1], d).astype(F32) for d in (1, 2, 3)]
+    resid = ((kept + sums[0]) + (sums[1] + sums[2])).astype(BF16)
+    mine = jnp.stack([resid] + [shift(resid, d) for d in (1, 2, 3)])
+    chip = lax.ppermute(mine, "tensor", CHIP_SWAP)
+    core = jnp.stack([lax.ppermute(mine, "tensor", CORE_SWAP), lax.ppermute(chip, "tensor", CORE_SWAP)])
+    normed, resid = call(
+        norm_all_body, "norm_all", (shape((4, 4, each, feature), BF16), shape((4, each, feature), BF16)),
+        (mine, chip, core, gains[1]), where, flops=rows * feature * 40, moved=rows * feature * 18,
+    )
+    normed = normed.reshape(4, rows, feature)
+    resid = resid.reshape(rows, feature)
+
+    acc = None
+    for c in range(CHUNKS):
+        own = hidden_chunk(where, normed, gate_weight, up_weight, c)
+        a1 = lax.ppermute(own, "batch", PAIRS_OUTER)
+        b1 = lax.ppermute(own, "batch", PAIRS_INNER)
+        a2 = lax.ppermute(b1, "batch", PAIRS_OUTER)
+        b2 = lax.ppermute(a1, "batch", PAIRS_INNER)
+        a3 = lax.ppermute(b2, "batch", PAIRS_OUTER)
+        pieces = [("one", [own], 1, c), ("one", [a1], 2, c), ("either", [b1, a2], 3, c), ("either", [b2, a3], 4, c)]
+        if c < CHUNKS - 1:
+            acc = down(where, acc, pieces, down_weight)
+        else:
+            acc = down(where, acc, pieces[:3], down_weight)
+            sent, held = down_last(where, acc, resid, slots, pieces[3:], down_weight)
+    core = lax.ppermute(sent, "tensor", CORE_SWAP)
+    chip = lax.ppermute((held[1] + core[1].astype(F32)).astype(BF16), "tensor", CHIP_SWAP)
+    return (held[0] + core[0].astype(F32) + chip.astype(F32)).astype(BF16)
+
+
+def per_device_packed(
+    frames, send_index, row_segment, attn_gain, q_weight, kv_weight, out_weight, ffn_gain, gate_weight,
+    up_weight, down_weight,
+):
+    b = lax.axis_index("batch")
+    t = lax.axis_index("tensor")
+    owned = frames.shape[0]
+    groups, capacity = send_index.shape[1:]
+    total = send_index.size
+    each = groups * capacity
+    pair = lax.bitwise_xor(b, 1)
+    where = jnp.stack([t, b, pair, jnp.where(b < 2, 2, 1), jnp.where(b < 2, 3, 0)]).astype(jnp.int32)
+
+    flat = send_index.reshape(total)
+    live = flat >= 0
+    count = jnp.sum(live.astype(jnp.int32))
+    most = jnp.maximum(count, lax.ppermute(count[None], "parts", [(0, 1), (1, 0)])[0])
+    outgoing = lax.dynamic_index_in_dim(send_index, b, 0, keepdims=False).reshape(each)
+    picked = jnp.take(frames, jnp.maximum(outgoing, 0), axis=0)
+    picked = jnp.where((outgoing >= 0)[:, None], picked, jnp.zeros_like(picked))
+    chip = lax.ppermute(picked, "tensor", CHIP_SWAP)
+    core = lax.ppermute(picked, "tensor", CORE_SWAP)
+    both = lax.ppermute(chip, "tensor", CORE_SWAP)
+
+    slot = jnp.arange(total, dtype=jnp.int32)
+    rank = jnp.sum((live[None, :] & (slot[None, :] < slot[:, None])).astype(jnp.int32), axis=1)
+    rank = jnp.where(live, rank, -1)
+    source = slot // each
+    at = source * owned + flat
+    looked = jnp.sum(
+        jnp.where(at[:, None] == jnp.arange(row_segment.shape[0], dtype=jnp.int32)[None, :], row_segment[None, :], 0),
+        axis=1,
+    )
+    keys = jnp.where(live, looked * groups + (slot // capacity) % groups, -1)
+    by_owner = rank.reshape(groups, each)
+    turned = (b - jnp.arange(4, dtype=jnp.int32)) % 4
+    ranks = by_owner[turned].reshape(1, total)
+    keys = keys.reshape(groups, each)[turned].reshape(1, total)
+    own_ranks = ranks[:, :each]
+    slots = rank.reshape(groups, groups, capacity).transpose(1, 0, 2).reshape(groups, each, 1)
+
+    gains = (attn_gain.reshape(4, -1), ffn_gain.reshape(4, -1))
+    normed = call(
+        norm_send_body, "norm_send", jax.ShapeDtypeStruct((4,) + picked.shape, BF16),
+        (picked, core, chip, both, gains[0]), where, flops=each * 5120 * 10, moved=each * 5120 * 4,
+    )
+    recv = [normed] + [shift(normed[d], d) for d in (1, 2, 3)]
+    weights = (q_weight, kv_weight, out_weight, gate_weight, up_weight, down_weight)
+    run = lambda rows: functools.partial(packed_layer, rows)
+    return lax.cond(
+        most <= 192, run(192), run(256), where, picked, recv, ranks, own_ranks, slots, keys, gains, weights
+    )
+
+
+def fits(mesh):
+    return mesh.shape["tensor"] == 4 and mesh.shape["batch"] == 4 and mesh.shape["parts"] == 2
+
+
 def solution(mesh):
     in_specs = (
         P(("parts", "batch"), "tensor"),
@@ -158,5 +549,5 @@
     )
     out_specs = P(("parts", "tensor"), "batch")
     return jax.shard_map(
-        per_device, mesh=mesh, in_specs=in_specs, out_specs=out_specs, check_vma=False
-    )
+        per_device_packed if fits(mesh) else per_device, mesh=mesh, in_specs=in_specs, out_specs=out_specs, check_vma=False
+    )

time: 709 us -> 222 us (0.31)
  waiting for transfers between devices: 596 us -> 81.3 us
  Pallas kernels: 0 us -> 64.3 us
  matrix products: 54 us -> 0 us
  starting transfers between devices: 6.71 us -> 59.9 us
  blocking collectives: 25.6 us -> 0 us
  between operations: 13.7 us -> 1.41 us
    all_gather x5 -> x0, waiting for transfers between devices: 541 us -> none  [the longest x1 181 us: per_device(): lax.all_gather(q_weight, 'batch', axis=0, tiled=True)]
    ppermute x0 -> x43, waiting for transfers between devices: none -> 81.3 us  [the longest x12 43.9 us: shift(): lax.ppermute(values, 'batch', [(i, (i + distance) % 4) for i in range(4)])]
    pallas_call x0 -> x14, Pallas kernels: none -> 64.3 us  [call(): pl.pallas_call(body, out_shape=out_shape, grid_spec=pltpu.PrefetchScalarG...]
    ppermute x0 -> x43, starting transfers between devices: none -> 59.9 us  [the longest x12 15.4 us: shift(): lax.ppermute(values, 'batch', [(i, (i + distance) % 4) for i in range(4)])]
    dot_general x7 -> x0, matrix products: 53.6 us -> none  [the longest x1 14.2 us: per_device(): jnp.dot(lax.all_gather(hidden, 'batch', axis=1, tiled=True), down_weight,...]
    reduce_scatter x2 -> x0, waiting for transfers between devices: 50 us -> none  [the longest x1 25.2 us: per_device(): lax.psum_scatter(projected, 'tensor', scatter_dimension=0, tiled=True)]
    all_gather x2 -> x0, blocking collectives: 25.6 us -> none  [the longest x1 17.7 us: per_device(): blocks = lax.all_gather(resid, 'batch', axis=0, tiled=True)]
  transfers between devices with their start and end apart: 8 -> 43, of which waited for: 8 -> 15; matrix products, arithmetic and copies ran while one was open for 2% -> 2% of each run, Pallas kernels for 0% -> 19%
where the time goes in v1:
time: 222 us; the launch traced here: 221 us
  waiting for transfers between devices  81.3 us (37%)
  Pallas kernels  64.3 us (29%)
  starting transfers between devices  59.9 us (27%)
  local copies, waits for them, and re-layouts  9.99 us (4%)
  other arithmetic  3.81 us (2%)
    pallas_call x14, Pallas kernels, call(): pl.pallas_call(body, out_shape=out_shape, grid_spec=pltpu.PrefetchScalarG...  64.3 us
    ppermute x12, waiting for transfers between devices, shift(): lax.ppermute(values, 'batch', [(i, (i + distance) % 4) for i in range(4)])  43.9 us
    ppermute x2, waiting for transfers between devices, packed_layer(): lax.ppermute((held[1] + core[1].astype(F32)).astype(BF16), 'tensor', CHIP...  16.5 us
    ppermute x12, starting transfers between devices, shift(): lax.ppermute(values, 'batch', [(i, (i + distance) % 4) for i in range(4)])  15.4 us
    ppermute x4, starting transfers between devices, packed_layer(): a1 = lax.ppermute(own, 'batch', PAIRS_OUTER)  11.9 us
    ppermute x4, starting transfers between devices, packed_layer(): a3 = lax.ppermute(b2, 'batch', PAIRS_OUTER)  11.5 us
    ppermute x1, waiting for transfers between devices, packed_layer(): chip = lax.ppermute(mine, 'tensor', CHIP_SWAP)  10.9 us
    unnamed x36, local copies, waits for them, and re-layouts  6.02 us
  transfers between devices with their start and end apart: 43, of which 15 were waited for; matrix products, arithmetic and copies ran while one was open for 2% of the time, Pallas kernels for 19%

profile of v1, /device:TPU:0, one launch (start us, length us, event | category | flops | bytes accessed | tf_op | source)
XLA Modules:
  0.0 221.5 jit_solution(11448125871745416784)
XLA Ops:
  0.0 0.8 broadcast_compare_fusion.1
  1.0 0.7 gather_fusion.4
  1.9 3.0 %collective-permute-start.74 = (bf16[64,1280]{1,0:T(8,128)(2,1)S(1)}, bf16[64,1280]{1,0:T(8,128)(2,1)S(1)}, u32[]{:S(2)}, u32[]{:S(2)}) collective-permute-start(bf16[64,1280]{1,0:T(8,128)(2,1)S(1)} %select_select_fusion.own), channel_id=1, source_target_pairs={{0,8},{8,0},{4,12},{12,4},{1,9},{9,1},{5,13},{13,5},{2,10},{10,2},... | collective-permute-start | bytes 491528 | tf_op jit(solution)/shard_map/ppermute | solution.py:498
  5.2 3.9 %collective-permute-done.74.chip = bf16[64,1280]{1,0:T(8,128)(2,1)S(1)} collective-permute-done((bf16[64,1280]{1,0:T(8,128)(2,1)S(1)}, bf16[64,1280]{1,0:T(8,128)(2,1)S(1)}, u32[]{:S(2)}, u32[]{:S(2)}) %collective-permute-start.74) | collective-permute-done | bytes 163872 | tf_op jit(solution)/shard_map/ppermute | solution.py:498
  9.7 1.8 collective-permute-start.72
  11.6 0.8 norm_send.1
  12.5 0.8 copy-done.17
  13.3 0.8 slice_bitcast_fusion.12
  14.1 3.6 %collective-permute-start.78 = (bf16[64,1280]{1,0:T(8,128)(2,1)}, bf16[64,1280]{1,0:T(8,128)(2,1)S(1)}, u32[]{:S(2)}, u32[]{:S(2)}) collective-permute-start(bf16[64,1280]{1,0:T(8,128)(2,1)} %get-tuple-element.592), channel_id=1, source_target_pairs={{0,3},{1,0},{2,1},{3,2},{4,7},{5,4},{6,5},{7,6},{8,11},{9,8},{10,9... | collective-permute-start | bytes 491528 | tf_op jit(solution)/shard_map/ppermute | solution.py:162
  17.7 1.0 collective-permute-start.76
  20.0 2.7 %collective-permute-done.78 = bf16[64,1280]{1,0:T(8,128)(2,1)S(1)} collective-permute-done((bf16[64,1280]{1,0:T(8,128)(2,1)}, bf16[64,1280]{1,0:T(8,128)(2,1)S(1)}, u32[]{:S(2)}, u32[]{:S(2)}) %collective-permute-start.78) | collective-permute-done | bytes 163872 | tf_op jit(solution)/shard_map/ppermute | solution.py:162
  22.6 9.5 %collective-permute-done.77 = bf16[64,1280]{1,0:T(8,128)(2,1)S(1)} collective-permute-done((bf16[64,1280]{1,0:T(8,128)(2,1)}, bf16[64,1280]{1,0:T(8,128)(2,1)S(1)}, u32[]{:S(2)}, u32[]{:S(2)}) %collective-permute-start.77) | collective-permute-done | bytes 163872 | tf_op jit(solution)/shard_map/ppermute | solution.py:162
  32.3 188.2 %conditional.6 = (bf16[64,1280]{1,0:T(8,128)(2,1)}) conditional(s32[]{:T(128)} %convert_element_type.132, (s32[4,4,16]{2,1,0:T(4,128)S(1)}, s32[4,64]{1,0:T(4,128)S(1)}, s32[256]{0:T(256)S(1)}, s32[4,64]{1,0:T(4,128)S(1)}, s32[4,1]{0,1:T(1,128)S(1)}, /*index=5*/s32[4,1]{0,1:T(1,128)S(1)}, s32[4,1]{0,1:T(1,128)S(1)}, s32[5]{0:T(128)S(1)}, ...), branch_computations={%region_2.6_spmd, %region_6.10_spmd} | conditional | flops 17843625984 | bytes 155954720
  33.8 4.0 %qkv.3 = (f32[192,512]{1,0:T(8,128)S(1)}, bf16[3,192,512]{2,1,0:T(8,128)(2,1)S(1)}) custom-call(s32[5]{0:T(128)S(1)} %get-tuple-element.318.where, bf16[4,64,1280]{2,1,0:T(8,128)(2,1)} %get-tuple-element.319.own, bf16[64,1280]{1,0:T(8,128)(2,1)} %copy-done.21, bf16[64,1280]{1,0:T(8,128)(2,1)} %copy-done.19, bf16[64,1280]{1,0:T(8,128)(2,1)S(1)} %get-tuple-element.322.third, ...), custom_call_target="tpu_custom_call" | custom-call | flops 754974720 | bytes 5084160 | tf_op jit(solution)/shard_map/cond/branch_1_fun/qkv/pallas_call | solution.py:173
  37.8 1.1 collective-permute-start.38
  38.9 1.9 collective-permute-start.37
  40.8 1.9 collective-permute-start.36
  44.8 12.9 %collective-permute-done.37.second = bf16[192,512]{1,0:T(8,128)(2,1)S(1)} collective-permute-done((bf16[192,512]{1,0:T(8,128)(2,1)S(1)}, bf16[192,512]{1,0:T(8,128)(2,1)S(1)}, u32[]{:S(2)}, u32[]{:S(2)}) %collective-permute-start.37) | collective-permute-done | bytes 196640 | tf_op jit(solution)/shard_map/cond/branch_1_fun/ppermute | solution.py:162
  57.7 3.9 %attend.3 = (bf16[2,192,1280]{2,1,0:T(8,128)(2,1)S(1)}, f32[2,192,1280]{2,1,0:T(8,128)S(1)}) custom-call(s32[5]{0:T(128)S(1)} %get-tuple-element.318.where, f32[192,512]{1,0:T(8,128)S(1)} %get-tuple-element.332.kept, bf16[192,512]{1,0:T(8,128)(2,1)S(1)} %collective-permute-done.36.first, bf16[192,512]{1,0:T(8,128)(2,1)S(1)} %collective-permute-done.37.second, ...), custom_call_target="tpu_custom_call" | custom-call | flops 503316480 | bytes 8381440 | tf_op jit(solution)/shard_map/cond/branch_1_fun/attend/pallas_call | solution.py:173
  61.6 2.6 %collective-permute-done.39.core = bf16[2,192,1280]{2,1,0:T(8,128)(2,1)S(1)} collective-permute-done((bf16[2,192,1280]{2,1,0:T(8,128)(2,1)S(1)}, bf16[2,192,1280]{2,1,0:T(8,128)(2,1)S(1)}, u32[]{:S(2)}, u32[]{:S(2)}) %collective-permute-start.39) | collective-permute-done | bytes 983072 | tf_op jit(solution)/shard_map/cond/branch_1_fun/ppermute | solution.py:439
  64.3 1.6 collective-permute-start.40
  65.8 11.8 %collective-permute-done.40.chip = bf16[192,1280]{1,0:T(8,128)(2,1)S(1)} collective-permute-done((bf16[192,1280]{1,0:T(8,128)(2,1)S(1)}, bf16[192,1280]{1,0:T(8,128)(2,1)S(1)}, u32[]{:S(2)}, u32[]{:S(2)}) %collective-permute-start.40) | collective-permute-done | bytes 491552 | tf_op jit(solution)/shard_map/cond/branch_1_fun/ppermute | solution.py:440
  77.6 0.9 gather_sum.3
  78.6 3.8 %collective-permute-start.43 = (bf16[48,1280]{1,0:T(8,128)(2,1)S(1)}, bf16[48,1280]{1,0:T(8,128)(2,1)S(1)}, u32[]{:S(2)}, u32[]{:S(2)}) collective-permute-start(bf16[48,1280]{1,0:T(8,128)(2,1)S(1)} %get-tuple-element.585), channel_id=1, source_target_pairs={{0,3},{1,0},{2,1},{3,2},{4,7},{5,4},{6,5},{7,6},{8,11},{9,8},{10,9... | collective-permute-start | bytes 368648 | tf_op jit(solution)/shard_map/cond/branch_1_fun/ppermute | solution.py:162
  82.4 4.2 %collective-permute-done.41 = bf16[48,1280]{1,0:T(8,128)(2,1)S(1)} collective-permute-done((bf16[48,1280]{1,0:T(8,128)(2,1)S(1)}, bf16[48,1280]{1,0:T(8,128)(2,1)S(1)}, u32[]{:S(2)}, u32[]{:S(2)}) %collective-permute-start.41) | collective-permute-done | bytes 122912 | tf_op jit(solution)/shard_map/cond/branch_1_fun/ppermute | solution.py:162
  86.7 4.8 %collective-permute-done.42 = bf16[48,1280]{1,0:T(8,128)(2,1)S(1)} collective-permute-done((bf16[48,1280]{1,0:T(8,128)(2,1)S(1)}, bf16[48,1280]{1,0:T(8,128)(2,1)S(1)}, u32[]{:S(2)}, u32[]{:S(2)}) %collective-permute-start.42) | collective-permute-done | bytes 122912 | tf_op jit(solution)/shard_map/cond/branch_1_fun/ppermute | solution.py:162
  91.6 1.4 collective-permute-start.46
  93.0 0.7 collective-permute-start.44
  93.7 3.6 %collective-permute-done.46 = bf16[48,1280]{1,0:T(8,128)(2,1)S(1)} collective-permute-done((bf16[48,1280]{1,0:T(8,128)(2,1)S(1)}, bf16[48,1280]{1,0:T(8,128)(2,1)S(1)}, u32[]{:S(2)}, u32[]{:S(2)}) %collective-permute-start.46) | collective-permute-done | bytes 122912 | tf_op jit(solution)/shard_map/cond/branch_1_fun/ppermute | solution.py:162
  97.3 5.8 %collective-permute-done.45 = bf16[48,1280]{1,0:T(8,128)(2,1)S(1)} collective-permute-done((bf16[48,1280]{1,0:T(8,128)(2,1)S(1)}, bf16[48,1280]{1,0:T(8,128)(2,1)S(1)}, u32[]{:S(2)}, u32[]{:S(2)}) %collective-permute-start.45) | collective-permute-done | bytes 122912 | tf_op jit(solution)/shard_map/cond/branch_1_fun/ppermute | solution.py:162
  103.2 1.6 collective-permute-start.47
  104.8 10.9 %collective-permute-done.47.chip = bf16[4,48,1280]{2,1,0:T(8,128)(2,1)S(1)} collective-permute-done((bf16[4,48,1280]{2,1,0:T(8,128)(2,1)S(1)}, bf16[4,48,1280]{2,1,0:T(8,128)(2,1)S(1)}, u32[]{:S(2)}, u32[]{:S(2)}) %collective-permute-start.47) | collective-permute-done | bytes 491552 | tf_op jit(solution)/shard_map/cond/branch_1_fun/ppermute | solution.py:450
  115.7 1.8 collective-permute-done.49
  117.6 1.6 norm_all.3
  119.3 6.5 %hidden.12.refs_0_ = bf16[192,512]{1,0:T(8,128)(2,1)S(1)} custom-call(s32[5]{0:T(128)S(1)} %get-tuple-element.318.where, bf16[4,192,1280]{2,1,0:T(8,128)(2,1)S(1)} %bitcast.79, bf16[5120,2048]{1,0:T(8,128)(2,1)} %get-tuple-element.403.gate_weight, bf16[5120,2048]{1,0:T(8,128)(2,1)} %get-tuple-element.405.up_weight), custom_call_target="tpu_custom_call" | custom-call | flops 2013265920 | bytes 10485760 | tf_op jit(solution)/shard_map/cond/branch_1_fun/hidden/pallas_call | solution.py:173
  125.8 0.7 collective-permute-start.51
  126.5 6.5 %hidden.13.refs_1_ = bf16[192,512]{1,0:T(8,128)(2,1)S(1)} custom-call(s32[5]{0:T(128)S(1)} %get-tuple-element.318.where, bf16[4,192,1280]{2,1,0:T(8,128)(2,1)S(1)} %bitcast.80, bf16[5120,2048]{1,0:T(8,128)(2,1)} %get-tuple-element.403.gate_weight, bf16[5120,2048]{1,0:T(8,128)(2,1)} %get-tuple-element.405.up_weight), custom_call_target="tpu_custom_call" | custom-call | flops 2013265920 | bytes 10485760 | tf_op jit(solution)/shard_map/cond/branch_1_fun/hidden/pallas_call | solution.py:173
  132.9 5.1 %collective-permute-start.50 = (bf16[192,512]{1,0:T(8,128)(2,1)S(1)}, bf16[192,512]{1,0:T(8,128)(2,1)S(1)}, u32[]{:S(2)}, u32[]{:S(2)}) collective-permute-start(bf16[192,512]{1,0:T(8,128)(2,1)S(1)} %hidden.12.refs_0_), channel_id=1, source_target_pairs={{0,1},{1,0},{2,3},{3,2},{4,5},{5,4},{6,7},{7,6},{8,9},{9,8},{10,11... | collective-permute-start | bytes 589832 | tf_op jit(solution)/shard_map/cond/branch_1_fun/ppermute | solution.py:462
  138.7 6.5 %hidden.14.refs_1_ = bf16[192,512]{1,0:T(8,128)(2,1)S(1)} custom-call(s32[5]{0:T(128)S(1)} %get-tuple-element.318.where, bf16[4,192,1280]{2,1,0:T(8,128)(2,1)S(1)} %bitcast.81, bf16[5120,2048]{1,0:T(8,128)(2,1)} %get-tuple-element.403.gate_weight, bf16[5120,2048]{1,0:T(8,128)(2,1)} %get-tuple-element.405.up_weight), custom_call_target="tpu_custom_call" | custom-call | flops 2013265920 | bytes 10485760 | tf_op jit(solution)/shard_map/cond/branch_1_fun/hidden/pallas_call | solution.py:173
  145.2 1.3 collective-permute-start.55
  147.2 3.3 %collective-permute-start.60 = (bf16[192,512]{1,0:T(8,128)(2,1)S(1)}, bf16[192,512]{1,0:T(8,128)(2,1)S(1)}, u32[]{:S(2)}, u32[]{:S(2)}) collective-permute-start(bf16[192,512]{1,0:T(8,128)(2,1)S(1)} %hidden.14.refs_1_), channel_id=1, source_target_pairs={{0,1},{1,0},{2,3},{3,2},{4,5},{5,4},{6,7},{7,6},{8,9},{9,8},{10,11... | collective-permute-start | bytes 589832 | tf_op jit(solution)/shard_map/cond/branch_1_fun/ppermute | solution.py:462
  150.6 6.5 %hidden.15.refs_1_ = bf16[192,512]{1,0:T(8,128)(2,1)S(1)} custom-call(s32[5]{0:T(128)S(1)} %get-tuple-element.318.where, bf16[4,192,1280]{2,1,0:T(8,128)(2,1)S(1)} %bitcast.82, bf16[5120,2048]{1,0:T(8,128)(2,1)} %get-tuple-element.403.gate_weight, bf16[5120,2048]{1,0:T(8,128)(2,1)} %get-tuple-element.405.up_weight), custom_call_target="tpu_custom_call" | custom-call | flops 2013265920 | bytes 10485760 | tf_op jit(solution)/shard_map/cond/branch_1_fun/hidden/pallas_call | solution.py:173
  157.8 2.1 collective-permute-start.65
  159.8 1.3 collective-permute-start.53
  161.8 1.9 collective-permute-start.52
  164.4 2.7 %collective-permute-start.57 = (bf16[192,512]{1,0:T(8,128)(2,1)S(1)}, bf16[192,512]{1,0:T(8,128)(2,1)S(1)}, u32[]{:S(2)}, u32[]{:S(2)}) collective-permute-start(bf16[192,512]{1,0:T(8,128)(2,1)S(1)} %collective-permute-done.56.refs_5_), channel_id=1, source_target_pairs={{0,1},{1,0},{2,3},{3,2},{4,5},{5,4},{6,7},{7,6},{8,9},{9,8},{10,11... | collective-permute-start | bytes 589832 | tf_op jit(solution)/shard_map/cond/branch_1_fun/ppermute | solution.py:464
  167.8 3.3 %collective-permute-start.54 = (bf16[192,512]{1,0:T(8,128)(2,1)}, bf16[192,512]{1,0:T(8,128)(2,1)}, u32[]{:S(2)}, u32[]{:S(2)}) collective-permute-start(bf16[192,512]{1,0:T(8,128)(2,1)} %collective-permute-done.53.refs_7_), channel_id=1, source_target_pairs={{0,1},{1,0},{2,3},{3,2},{4,5},{5,4},{6,7},{7,6},{8,9},{9,8},{10,11... | collective-permute-start | bytes 589832 | tf_op jit(solution)/shard_map/cond/branch_1_fun/ppermute | solution.py:466
  171.8 0.9 collective-permute-start.68
  172.8 2.7 %collective-permute-start.59 = (bf16[192,512]{1,0:T(8,128)(2,1)S(1)}, bf16[192,512]{1,0:T(8,128)(2,1)}, u32[]{:S(2)}, u32[]{:S(2)}) collective-permute-start(bf16[192,512]{1,0:T(8,128)(2,1)S(1)} %collective-permute-done.58.refs_8_), channel_id=1, source_target_pairs={{0,1},{1,0},{2,3},{3,2},{4,5},{5,4},{6,7},{7,6},{8,9},{9,8},{10,11... | collective-permute-start | bytes 589832 | tf_op jit(solution)/shard_map/cond/branch_1_fun/ppermute | solution.py:466
  175.7 3.7 %collective-permute-start.64 = (bf16[192,512]{1,0:T(8,128)(2,1)S(1)}, bf16[192,512]{1,0:T(8,128)(2,1)}, u32[]{:S(2)}, u32[]{:S(2)}) collective-permute-start(bf16[192,512]{1,0:T(8,128)(2,1)S(1)} %collective-permute-done.63.refs_8_), channel_id=1, source_target_pairs={{0,1},{1,0},{2,3},{3,2},{4,5},{5,4},{6,7},{7,6},{8,9},{9,8},{10,11... | collective-permute-start | bytes 589832 | tf_op jit(solution)/shard_map/cond/branch_1_fun/ppermute | solution.py:466
  180.1 0.9 copy-done.11
  181.0 0.9 copy-done.13
  181.9 0.9 copy-done.15
  182.8 5.7 %down.12.refs_0_ = f32[192,1280]{1,0:T(8,128)S(1)} custom-call(s32[5]{0:T(128)S(1)} %get-tuple-element.318.where, bf16[192,512]{1,0:T(8,128)(2,1)S(1)} %hidden.12.refs_0_, bf16[8192,1280]{1,0:T(8,128)(2,1)} %get-tuple-element.407.refs_1_.refs_3_.refs_6_.refs_9_.refs_2_.refs_4_.refs_7_.refs_10_, bf16[192,512]{1,0:T(8,128)(2,1)S(1)} %copy-done.13, ...), custom_call_target="tpu_custom_call" | custom-call | flops 1006632960 | bytes 5242880 | tf_op jit(solution)/shard_map/cond/branch_1_fun/down/pallas_call | solution.py:173
  188.5 1.7 collective-permute-start.69
  190.2 5.6 %down.13.refs_0_ = f32[192,1280]{1,0:T(8,128)S(1)} custom-call(s32[5]{0:T(128)S(1)} %get-tuple-element.318.where, f32[192,1280]{1,0:T(8,128)S(1)} %down.12.refs_0_, bf16[192,512]{1,0:T(8,128)(2,1)S(1)} %hidden.13.refs_1_, ...), custom_call_target="tpu_custom_call", output_to_operand_aliasing={{}: (1, {})} | custom-call | flops 1006632960 | bytes 5242880 | tf_op jit(solution)/shard_map/cond/branch_1_fun/down/pallas_call | solution.py:173
  195.9 5.7 %down.14.refs_0_ = f32[192,1280]{1,0:T(8,128)S(1)} custom-call(s32[5]{0:T(128)S(1)} %get-tuple-element.318.where, f32[192,1280]{1,0:T(8,128)S(1)} %down.13.refs_0_, bf16[192,512]{1,0:T(8,128)(2,1)S(1)} %hidden.14.refs_1_, ...), custom_call_target="tpu_custom_call", output_to_operand_aliasing={{}: (1, {})} | custom-call | flops 1006632960 | bytes 5242880 | tf_op jit(solution)/shard_map/cond/branch_1_fun/down/pallas_call | solution.py:173
  201.6 5.1 %down.15.acc = f32[192,1280]{1,0:T(8,128)S(1)} custom-call(s32[5]{0:T(128)S(1)} %get-tuple-element.318.where, f32[192,1280]{1,0:T(8,128)S(1)} %down.14.refs_0_, bf16[192,512]{1,0:T(8,128)(2,1)S(1)} %hidden.15.refs_1_, ...), custom_call_target="tpu_custom_call", output_to_operand_aliasing={{}: (1, {})} | custom-call | flops 754974720 | bytes 3932160 | tf_op jit(solution)/shard_map/cond/branch_1_fun/down/pallas_call | solution.py:173
  206.7 5.0 %down_last.3 = (bf16[2,64,1280]{2,1,0:T(8,128)(2,1)S(1)}, f32[2,64,1280]{2,1,0:T(8,128)S(1)}) custom-call(s32[5]{0:T(128)S(1)} %get-tuple-element.318.where, f32[192,1280]{1,0:T(8,128)S(1)} %down.15.acc, bf16[192,1280]{1,0:T(8,128)(2,1)S(1)} %bitcast.84, s32[4,64,1]{2,1,0:T(8,128)S(1)} %reshape.302.slots, ...), custom_call_target="tpu_custom_call" | custom-call | flops 251658240 | bytes 1310720 | tf_op jit(solution)/shard_map/cond/branch_1_fun/down_last/pallas_call | solution.py:173
  211.9 1.6 collective-permute-done.70
  213.5 1.5 collective-permute-start.71
  215.0 4.8 %collective-permute-done.71 = bf16[64,1280]{1,0:T(8,128)(2,1)S(1)} collective-permute-done((bf16[64,1280]{1,0:T(8,128)(2,1)S(1)}, bf16[64,1280]{1,0:T(8,128)(2,1)S(1)}, u32[]{:S(2)}, u32[]{:S(2)}) %collective-permute-start.71) | collective-permute-done | bytes 163872 | tf_op jit(solution)/shard_map/cond/branch_1_fun/ppermute | solution.py:474
  219.8 0.7 bitcast_add_fusion.1
  220.5 0.9 copy-done.1
  (134 shorter events, 11.0 us)
Async XLA Ops:
  0.0 1.0 copy-start
  0.0 4.9 %copy-start.22 = (s32[4,4,16]{2,1,0:T(4,128)S(1)}, s32[4,4,16]{2,1,0:T(4,128)}, u32[]{:S(2)}) copy-start(s32[4,4,16]{2,1,0:T(4,128)} %param.14) | copy-start | bytes 3076
  0.0 11.5 %copy-start.26 = (f32[5120]{0:T(1024)S(1)}, f32[5120]{0:T(1024)}, u32[]{:S(2)}) copy-start(f32[5120]{0:T(1024)} %param.16) | copy-start | bytes 61444
  1.9 7.2 %collective-permute-start.74 = (bf16[64,1280]{1,0:T(8,128)(2,1)S(1)}, bf16[64,1280]{1,0:T(8,128)(2,1)S(1)}, u32[]{:S(2)}, u32[]{:S(2)}) collective-permute-start(bf16[64,1280]{1,0:T(8,128)(2,1)S(1)} %select_select_fusion.own), channel_id=1, source_target_pairs={{0,8},{8,0},{4,12},{12,4},{1,9},{9,1},{5,13},{13,5},{2,10},{10,2},... | collective-permute-start | bytes 491528 | tf_op jit(solution)/shard_map/ppermute | solution.py:498
  4.9 6.7 %collective-permute-start.73 = (bf16[64,1280]{1,0:T(8,128)(2,1)S(1)}, bf16[64,1280]{1,0:T(8,128)(2,1)S(1)}, u32[]{:S(2)}, u32[]{:S(2)}) collective-permute-start(bf16[64,1280]{1,0:T(8,128)(2,1)S(1)} %select_select_fusion.own), channel_id=1, source_target_pairs={{0,4},{4,0},{8,12},{12,8},{1,5},{5,1},{9,13},{13,9},{2,6},{6,2},{1... | collective-permute-start | bytes 491528 | tf_op jit(solution)/shard_map/ppermute | solution.py:499
  9.1 2.5 %collective-permute-start.75 = (bf16[64,1280]{1,0:T(8,128)(2,1)S(1)}, bf16[64,1280]{1,0:T(8,128)(2,1)S(1)}, u32[]{:S(2)}, u32[]{:S(2)}) collective-permute-start(bf16[64,1280]{1,0:T(8,128)(2,1)S(1)} %collective-permute-done.74.chip), channel_id=1, source_target_pairs={{0,4},{4,0},{8,12},{12,8},{1,5},{5,1},{9,13},{13,9},{2,6},{6,2},{1... | collective-permute-start | bytes 491528 | tf_op jit(solution)/shard_map/ppermute | solution.py:500
  9.7 9.0 %collective-permute-start.72 = (s32[1]{0:T(128)}, s32[1]{0:T(128)}, u32[]{:S(2)}, u32[]{:S(2)}) collective-permute-start(s32[1]{0:T(128)} %bitcast.40), channel_id=1, source_target_pairs={{0,16},{16,0},{1,17},{17,1},{2,18},{18,2},{3,19},{19,3},{4,20},{20... | collective-permute-start | bytes 20 | tf_op jit(solution)/shard_map/ppermute | solution.py:494
  11.6 20.7 %copy-start.16 = (bf16[1280,1024]{1,0:T(8,128)(2,1)S(1)}, bf16[1280,1024]{1,0:T(8,128)(2,1)}, u32[]{:S(2)}) copy-start(bf16[1280,1024]{1,0:T(8,128)(2,1)} %param.17) | copy-start | bytes 7864324
  11.6 20.7 %copy-start.23 = (f32[5120]{0:T(1024)S(1)}, f32[5120]{0:T(1024)}, u32[]{:S(2)}) copy-start(f32[5120]{0:T(1024)} %param.20) | copy-start | bytes 61444
  11.6 20.7 %copy-start.27 = (s32[320]{0:T(512)S(1)}, s32[320]{0:T(512)}, u32[]{:S(2)}) copy-start(s32[320]{0:T(512)} %param.15) | copy-start | bytes 3844
  12.5 0.9 copy-start.17
  14.1 8.6 %collective-permute-start.78 = (bf16[64,1280]{1,0:T(8,128)(2,1)}, bf16[64,1280]{1,0:T(8,128)(2,1)S(1)}, u32[]{:S(2)}, u32[]{:S(2)}) collective-permute-start(bf16[64,1280]{1,0:T(8,128)(2,1)} %get-tuple-element.592), channel_id=1, source_target_pairs={{0,3},{1,0},{2,1},{3,2},{4,7},{5,4},{6,5},{7,6},{8,11},{9,8},{10,9... | collective-permute-start | bytes 491528 | tf_op jit(solution)/shard_map/ppermute | solution.py:162
  17.7 14.5 %collective-permute-start.77 = (bf16[64,1280]{1,0:T(8,128)(2,1)}, bf16[64,1280]{1,0:T(8,128)(2,1)S(1)}, u32[]{:S(2)}, u32[]{:S(2)}) collective-permute-start(bf16[64,1280]{1,0:T(8,128)(2,1)} %get-tuple-element.593), channel_id=1, source_target_pairs={{0,2},{1,3},{2,0},{3,1},{4,6},{5,7},{6,4},{7,5},{8,10},{9,11},{10,... | collective-permute-start | bytes 491528 | tf_op jit(solution)/shard_map/ppermute | solution.py:162
  17.7 14.5 %collective-permute-start.76 = (bf16[64,1280]{1,0:T(8,128)(2,1)S(1)}, bf16[64,1280]{1,0:T(8,128)(2,1)S(1)}, u32[]{:S(2)}, u32[]{:S(2)}) collective-permute-start(bf16[64,1280]{1,0:T(8,128)(2,1)S(1)} %get-tuple-element.594), channel_id=1, source_target_pairs={{0,1},{1,2},{2,3},{3,0},{4,5},{5,6},{6,7},{7,4},{8,9},{9,10},{10,1... | collective-permute-start | bytes 491528 | tf_op jit(solution)/shard_map/ppermute | solution.py:162
  32.5 0.6 copy-start.24
  32.6 1.3 copy-start.19
  32.6 1.3 copy-start.21
  37.8 7.0 %collective-permute-start.38 = (bf16[192,512]{1,0:T(8,128)(2,1)S(1)}, bf16[192,512]{1,0:T(8,128)(2,1)S(1)}, u32[]{:S(2)}, u32[]{:S(2)}) collective-permute-start(bf16[192,512]{1,0:T(8,128)(2,1)S(1)} %get-tuple-element.581), channel_id=1, source_target_pairs={{0,3},{1,0},{2,1},{3,2},{4,7},{5,4},{6,5},{7,6},{8,11},{9,8},{10,9... | collective-permute-start | bytes 589832 | tf_op jit(solution)/shard_map/cond/branch_1_fun/ppermute | solution.py:162
  38.9 18.8 %collective-permute-start.37 = (bf16[192,512]{1,0:T(8,128)(2,1)S(1)}, bf16[192,512]{1,0:T(8,128)(2,1)S(1)}, u32[]{:S(2)}, u32[]{:S(2)}) collective-permute-start(bf16[192,512]{1,0:T(8,128)(2,1)S(1)} %get-tuple-element.582), channel_id=1, source_target_pairs={{0,2},{1,3},{2,0},{3,1},{4,6},{5,7},{6,4},{7,5},{8,10},{9,11},{10,... | collective-permute-start | bytes 589832 | tf_op jit(solution)/shard_map/cond/branch_1_fun/ppermute | solution.py:162
  40.8 16.9 %collective-permute-start.36 = (bf16[192,512]{1,0:T(8,128)(2,1)S(1)}, bf16[192,512]{1,0:T(8,128)(2,1)S(1)}, u32[]{:S(2)}, u32[]{:S(2)}) collective-permute-start(bf16[192,512]{1,0:T(8,128)(2,1)S(1)} %get-tuple-element.583), channel_id=1, source_target_pairs={{0,1},{1,2},{2,3},{3,0},{4,5},{5,6},{6,7},{7,4},{8,9},{9,10},{10,1... | collective-permute-start | bytes 589832 | tf_op jit(solution)/shard_map/cond/branch_1_fun/ppermute | solution.py:162
  61.6 2.6 %collective-permute-start.39 = (bf16[2,192,1280]{2,1,0:T(8,128)(2,1)S(1)}, bf16[2,192,1280]{2,1,0:T(8,128)(2,1)S(1)}, u32[]{:S(2)}, u32[]{:S(2)}) collective-permute-start(bf16[2,192,1280]{2,1,0:T(8,128)(2,1)S(1)} %get-tuple-element.344), channel_id=1, source_target_pairs={{0,4},{4,0},{8,12},{12,8},{1,5},{5,1},{9,13},{13,9},{2,6},{6,2},{1... | collective-permute-start | bytes 2949128 | tf_op jit(solution)/shard_map/cond/branch_1_fun/ppermute | solution.py:439
  64.3 13.3 %collective-permute-start.40 = (bf16[192,1280]{1,0:T(8,128)(2,1)S(1)}, bf16[192,1280]{1,0:T(8,128)(2,1)S(1)}, u32[]{:S(2)}, u32[]{:S(2)}) collective-permute-start(bf16[192,1280]{1,0:T(8,128)(2,1)S(1)} %fusion.9), channel_id=1, source_target_pairs={{0,8},{8,0},{4,12},{12,4},{1,9},{9,1},{5,13},{13,5},{2,10},{10,2},... | collective-permute-start | bytes 1474568 | tf_op jit(solution)/shard_map/cond/branch_1_fun/ppermute | solution.py:440
  78.5 37.2 %copy-start.25 = (f32[5120]{0:T(1024)S(1)}, f32[5120]{0:T(1024)}, u32[]{:S(2)}) copy-start(f32[5120]{0:T(1024)} %copy-done.24) | copy-start | bytes 61444
  78.6 8.1 %collective-permute-start.41 = (bf16[48,1280]{1,0:T(8,128)(2,1)S(1)}, bf16[48,1280]{1,0:T(8,128)(2,1)S(1)}, u32[]{:S(2)}, u32[]{:S(2)}) collective-permute-start(bf16[48,1280]{1,0:T(8,128)(2,1)S(1)} %get-tuple-element.584), channel_id=1, source_target_pairs={{0,1},{1,2},{2,3},{3,0},{4,5},{5,6},{6,7},{7,4},{8,9},{9,10},{10,1... | collective-permute-start | bytes 368648 | tf_op jit(solution)/shard_map/cond/branch_1_fun/ppermute | solution.py:162
  78.6 8.0 %collective-permute-start.43 = (bf16[48,1280]{1,0:T(8,128)(2,1)S(1)}, bf16[48,1280]{1,0:T(8,128)(2,1)S(1)}, u32[]{:S(2)}, u32[]{:S(2)}) collective-permute-start(bf16[48,1280]{1,0:T(8,128)(2,1)S(1)} %get-tuple-element.585), channel_id=1, source_target_pairs={{0,3},{1,0},{2,1},{3,2},{4,7},{5,4},{6,5},{7,6},{8,11},{9,8},{10,9... | collective-permute-start | bytes 368648 | tf_op jit(solution)/shard_map/cond/branch_1_fun/ppermute | solution.py:162
  82.4 9.1 %collective-permute-start.42 = (bf16[48,1280]{1,0:T(8,128)(2,1)S(1)}, bf16[48,1280]{1,0:T(8,128)(2,1)S(1)}, u32[]{:S(2)}, u32[]{:S(2)}) collective-permute-start(bf16[48,1280]{1,0:T(8,128)(2,1)S(1)} %get-tuple-element.586), channel_id=1, source_target_pairs={{0,2},{1,3},{2,0},{3,1},{4,6},{5,7},{6,4},{7,5},{8,10},{9,11},{10,... | collective-permute-start | bytes 368648 | tf_op jit(solution)/shard_map/cond/branch_1_fun/ppermute | solution.py:162
  91.6 5.7 %collective-permute-start.46 = (bf16[48,1280]{1,0:T(8,128)(2,1)S(1)}, bf16[48,1280]{1,0:T(8,128)(2,1)S(1)}, u32[]{:S(2)}, u32[]{:S(2)}) collective-permute-start(bf16[48,1280]{1,0:T(8,128)(2,1)S(1)} %add_convert_fusion.6), channel_id=1, source_target_pairs={{0,3},{1,0},{2,1},{3,2},{4,7},{5,4},{6,5},{7,6},{8,11},{9,8},{10,9... | collective-permute-start | bytes 368648 | tf_op jit(solution)/shard_map/cond/branch_1_fun/ppermute | solution.py:162
  93.0 10.2 %collective-permute-start.45 = (bf16[48,1280]{1,0:T(8,128)(2,1)S(1)}, bf16[48,1280]{1,0:T(8,128)(2,1)S(1)}, u32[]{:S(2)}, u32[]{:S(2)}) collective-permute-start(bf16[48,1280]{1,0:T(8,128)(2,1)S(1)} %add_convert_fusion.6), channel_id=1, source_target_pairs={{0,2},{1,3},{2,0},{3,1},{4,6},{5,7},{6,4},{7,5},{8,10},{9,11},{10,... | collective-permute-start | bytes 368648 | tf_op jit(solution)/shard_map/cond/branch_1_fun/ppermute | solution.py:162
  93.0 10.2 %collective-permute-start.44 = (bf16[48,1280]{1,0:T(8,128)(2,1)S(1)}, bf16[48,1280]{1,0:T(8,128)(2,1)S(1)}, u32[]{:S(2)}, u32[]{:S(2)}) collective-permute-start(bf16[48,1280]{1,0:T(8,128)(2,1)S(1)} %add_convert_fusion.6), channel_id=1, source_target_pairs={{0,1},{1,2},{2,3},{3,0},{4,5},{5,6},{6,7},{7,4},{8,9},{9,10},{10,1... | collective-permute-start | bytes 368648 | tf_op jit(solution)/shard_map/cond/branch_1_fun/ppermute | solution.py:162
  103.2 12.5 %collective-permute-start.47 = (bf16[4,48,1280]{2,1,0:T(8,128)(2,1)S(1)}, bf16[4,48,1280]{2,1,0:T(8,128)(2,1)S(1)}, u32[]{:S(2)}, u32[]{:S(2)}) collective-permute-start(bf16[4,48,1280]{2,1,0:T(8,128)(2,1)S(1)} %pad_maximum_fusion.5.own), channel_id=1, source_target_pairs={{0,8},{8,0},{4,12},{12,4},{1,9},{9,1},{5,13},{13,5},{2,10},{10,2},... | collective-permute-start | bytes 1474568 | tf_op jit(solution)/shard_map/cond/branch_1_fun/ppermute | solution.py:450
  104.8 10.9 %collective-permute-start.48 = (bf16[4,48,1280]{2,1,0:T(8,128)(2,1)S(1)}, bf16[4,48,1280]{2,1,0:T(8,128)(2,1)S(1)}, u32[]{:S(2)}, u32[]{:S(2)}) collective-permute-start(bf16[4,48,1280]{2,1,0:T(8,128)(2,1)S(1)} %pad_maximum_fusion.5.own), channel_id=1, source_target_pairs={{0,4},{4,0},{8,12},{12,8},{1,5},{5,1},{9,13},{13,9},{2,6},{6,2},{1... | collective-permute-start | bytes 1474568 | tf_op jit(solution)/shard_map/cond/branch_1_fun/ppermute | solution.py:451
  115.7 1.9 collective-permute-start.49
  125.8 21.5 %collective-permute-start.51 = (bf16[192,512]{1,0:T(8,128)(2,1)S(1)}, bf16[192,512]{1,0:T(8,128)(2,1)S(1)}, u32[]{:S(2)}, u32[]{:S(2)}) collective-permute-start(bf16[192,512]{1,0:T(8,128)(2,1)S(1)} %hidden.12.refs_0_), channel_id=1, source_target_pairs={{0,0},{1,2},{2,1},{3,3},{4,4},{5,6},{6,5},{7,7},{8,8},{9,10},{10,9... | collective-permute-start | bytes 589832 | tf_op jit(solution)/shard_map/cond/branch_1_fun/ppermute | solution.py:463
  132.9 24.1 %collective-permute-start.50 = (bf16[192,512]{1,0:T(8,128)(2,1)S(1)}, bf16[192,512]{1,0:T(8,128)(2,1)S(1)}, u32[]{:S(2)}, u32[]{:S(2)}) collective-permute-start(bf16[192,512]{1,0:T(8,128)(2,1)S(1)} %hidden.12.refs_0_), channel_id=1, source_target_pairs={{0,1},{1,0},{2,3},{3,2},{4,5},{5,4},{6,7},{7,6},{8,9},{9,8},{10,11... | collective-permute-start | bytes 589832 | tf_op jit(solution)/shard_map/cond/branch_1_fun/ppermute | solution.py:462
  138.1 19.7 %collective-permute-start.56 = (bf16[192,512]{1,0:T(8,128)(2,1)S(1)}, bf16[192,512]{1,0:T(8,128)(2,1)S(1)}, u32[]{:S(2)}, u32[]{:S(2)}) collective-permute-start(bf16[192,512]{1,0:T(8,128)(2,1)S(1)} %hidden.13.refs_1_), channel_id=1, source_target_pairs={{0,0},{1,2},{2,1},{3,3},{4,4},{5,6},{6,5},{7,7},{8,8},{9,10},{10,9... | collective-permute-start | bytes 589832 | tf_op jit(solution)/shard_map/cond/branch_1_fun/ppermute | solution.py:463
  145.2 14.6 %collective-permute-start.55 = (bf16[192,512]{1,0:T(8,128)(2,1)S(1)}, bf16[192,512]{1,0:T(8,128)(2,1)S(1)}, u32[]{:S(2)}, u32[]{:S(2)}) collective-permute-start(bf16[192,512]{1,0:T(8,128)(2,1)S(1)} %hidden.13.refs_1_), channel_id=1, source_target_pairs={{0,1},{1,0},{2,3},{3,2},{4,5},{5,4},{6,7},{7,6},{8,9},{9,8},{10,11... | collective-permute-start | bytes 589832 | tf_op jit(solution)/shard_map/cond/branch_1_fun/ppermute | solution.py:462
  146.6 15.3 %collective-permute-start.61 = (bf16[192,512]{1,0:T(8,128)(2,1)S(1)}, bf16[192,512]{1,0:T(8,128)(2,1)S(1)}, u32[]{:S(2)}, u32[]{:S(2)}) collective-permute-start(bf16[192,512]{1,0:T(8,128)(2,1)S(1)} %hidden.14.refs_1_), channel_id=1, source_target_pairs={{0,0},{1,2},{2,1},{3,3},{4,4},{5,6},{6,5},{7,7},{8,8},{9,10},{10,9... | collective-permute-start | bytes 589832 | tf_op jit(solution)/shard_map/cond/branch_1_fun/ppermute | solution.py:463
  147.2 14.6 %copy-start.10 = (bf16[192,512]{1,0:T(8,128)(2,1)}, bf16[192,512]{1,0:T(8,128)(2,1)S(1)}, u32[]{:S(2)}) copy-start(bf16[192,512]{1,0:T(8,128)(2,1)S(1)} %collective-permute-done.51.refs_4_) | copy-start | bytes 589828
  147.2 16.5 %collective-permute-start.60 = (bf16[192,512]{1,0:T(8,128)(2,1)S(1)}, bf16[192,512]{1,0:T(8,128)(2,1)S(1)}, u32[]{:S(2)}, u32[]{:S(2)}) collective-permute-start(bf16[192,512]{1,0:T(8,128)(2,1)S(1)} %hidden.14.refs_1_), channel_id=1, source_target_pairs={{0,1},{1,0},{2,3},{3,2},{4,5},{5,4},{6,7},{7,6},{8,9},{9,8},{10,11... | collective-permute-start | bytes 589832 | tf_op jit(solution)/shard_map/cond/branch_1_fun/ppermute | solution.py:462
  157.1 7.3 %collective-permute-start.66 = (bf16[192,512]{1,0:T(8,128)(2,1)S(1)}, bf16[192,512]{1,0:T(8,128)(2,1)S(1)}, u32[]{:S(2)}, u32[]{:S(2)}) collective-permute-start(bf16[192,512]{1,0:T(8,128)(2,1)S(1)} %hidden.15.refs_1_), channel_id=1, source_target_pairs={{0,0},{1,2},{2,1},{3,3},{4,4},{5,6},{6,5},{7,7},{8,8},{9,10},{10,9... | collective-permute-start | bytes 589832 | tf_op jit(solution)/shard_map/cond/branch_1_fun/ppermute | solution.py:463
  157.8 9.4 %collective-permute-start.65 = (bf16[192,512]{1,0:T(8,128)(2,1)S(1)}, bf16[192,512]{1,0:T(8,128)(2,1)S(1)}, u32[]{:S(2)}, u32[]{:S(2)}) collective-permute-start(bf16[192,512]{1,0:T(8,128)(2,1)S(1)} %hidden.15.refs_1_), channel_id=1, source_target_pairs={{0,1},{1,0},{2,3},{3,2},{4,5},{5,4},{6,7},{7,6},{8,9},{9,8},{10,11... | collective-permute-start | bytes 589832 | tf_op jit(solution)/shard_map/cond/branch_1_fun/ppermute | solution.py:462
  159.8 8.0 %collective-permute-start.53 = (bf16[192,512]{1,0:T(8,128)(2,1)S(1)}, bf16[192,512]{1,0:T(8,128)(2,1)}, u32[]{:S(2)}, u32[]{:S(2)}) collective-permute-start(bf16[192,512]{1,0:T(8,128)(2,1)S(1)} %collective-permute-done.50.refs_2_), channel_id=1, source_target_pairs={{0,0},{1,2},{2,1},{3,3},{4,4},{5,6},{6,5},{7,7},{8,8},{9,10},{10,9... | collective-permute-start | bytes 589832 | tf_op jit(solution)/shard_map/cond/branch_1_fun/ppermute | solution.py:465
  161.2 0.7 copy-start.12
  161.8 9.3 %collective-permute-start.52 = (bf16[192,512]{1,0:T(8,128)(2,1)S(1)}, bf16[192,512]{1,0:T(8,128)(2,1)S(1)}, u32[]{:S(2)}, u32[]{:S(2)}) collective-permute-start(bf16[192,512]{1,0:T(8,128)(2,1)S(1)} %collective-permute-done.51.refs_4_), channel_id=1, source_target_pairs={{0,1},{1,0},{2,3},{3,2},{4,5},{5,4},{6,7},{7,6},{8,9},{9,8},{10,11... | collective-permute-start | bytes 589832 | tf_op jit(solution)/shard_map/cond/branch_1_fun/ppermute | solution.py:464
  163.7 9.0 %collective-permute-start.58 = (bf16[192,512]{1,0:T(8,128)(2,1)S(1)}, bf16[192,512]{1,0:T(8,128)(2,1)S(1)}, u32[]{:S(2)}, u32[]{:S(2)}) collective-permute-start(bf16[192,512]{1,0:T(8,128)(2,1)S(1)} %collective-permute-done.55.refs_3_), channel_id=1, source_target_pairs={{0,0},{1,2},{2,1},{3,3},{4,4},{5,6},{6,5},{7,7},{8,8},{9,10},{10,9... | collective-permute-start | bytes 589832 | tf_op jit(solution)/shard_map/cond/branch_1_fun/ppermute | solution.py:465
  164.4 11.1 %collective-permute-start.57 = (bf16[192,512]{1,0:T(8,128)(2,1)S(1)}, bf16[192,512]{1,0:T(8,128)(2,1)S(1)}, u32[]{:S(2)}, u32[]{:S(2)}) collective-permute-start(bf16[192,512]{1,0:T(8,128)(2,1)S(1)} %collective-permute-done.56.refs_5_), channel_id=1, source_target_pairs={{0,1},{1,0},{2,3},{3,2},{4,5},{5,4},{6,7},{7,6},{8,9},{9,8},{10,11... | collective-permute-start | bytes 589832 | tf_op jit(solution)/shard_map/cond/branch_1_fun/ppermute | solution.py:464
  167.1 8.6 %collective-permute-start.63 = (bf16[192,512]{1,0:T(8,128)(2,1)S(1)}, bf16[192,512]{1,0:T(8,128)(2,1)S(1)}, u32[]{:S(2)}, u32[]{:S(2)}) collective-permute-start(bf16[192,512]{1,0:T(8,128)(2,1)S(1)} %collective-permute-done.60.refs_3_), channel_id=1, source_target_pairs={{0,0},{1,2},{2,1},{3,3},{4,4},{5,6},{6,5},{7,7},{8,8},{9,10},{10,9... | collective-permute-start | bytes 589832 | tf_op jit(solution)/shard_map/cond/branch_1_fun/ppermute | solution.py:465
  167.8 11.8 %collective-permute-start.54 = (bf16[192,512]{1,0:T(8,128)(2,1)}, bf16[192,512]{1,0:T(8,128)(2,1)}, u32[]{:S(2)}, u32[]{:S(2)}) collective-permute-start(bf16[192,512]{1,0:T(8,128)(2,1)} %collective-permute-done.53.refs_7_), channel_id=1, source_target_pairs={{0,1},{1,0},{2,3},{3,2},{4,5},{5,4},{6,7},{7,6},{8,9},{9,8},{10,11... | collective-permute-start | bytes 589832 | tf_op jit(solution)/shard_map/cond/branch_1_fun/ppermute | solution.py:466
  171.2 0.7 copy-start.14
  171.8 16.7 %collective-permute-start.68 = (bf16[192,512]{1,0:T(8,128)(2,1)S(1)}, bf16[192,512]{1,0:T(8,128)(2,1)S(1)}, u32[]{:S(2)}, u32[]{:S(2)}) collective-permute-start(bf16[192,512]{1,0:T(8,128)(2,1)S(1)} %collective-permute-done.65.refs_3_), channel_id=1, source_target_pairs={{0,0},{1,2},{2,1},{3,3},{4,4},{5,6},{6,5},{7,7},{8,8},{9,10},{10,9... | collective-permute-start | bytes 589832 | tf_op jit(solution)/shard_map/cond/branch_1_fun/ppermute | solution.py:465
  172.8 17.5 %collective-permute-start.59 = (bf16[192,512]{1,0:T(8,128)(2,1)S(1)}, bf16[192,512]{1,0:T(8,128)(2,1)}, u32[]{:S(2)}, u32[]{:S(2)}) collective-permute-start(bf16[192,512]{1,0:T(8,128)(2,1)S(1)} %collective-permute-done.58.refs_8_), channel_id=1, source_target_pairs={{0,1},{1,0},{2,3},{3,2},{4,5},{5,4},{6,7},{7,6},{8,9},{9,8},{10,11... | collective-permute-start | bytes 589832 | tf_op jit(solution)/shard_map/cond/branch_1_fun/ppermute | solution.py:466
  175.5 20.4 %collective-permute-start.62 = (bf16[192,512]{1,0:T(8,128)(2,1)S(1)}, bf16[192,512]{1,0:T(8,128)(2,1)}, u32[]{:S(2)}, u32[]{:S(2)}) collective-permute-start(bf16[192,512]{1,0:T(8,128)(2,1)S(1)} %collective-permute-done.61.refs_5_), channel_id=1, source_target_pairs={{0,1},{1,0},{2,3},{3,2},{4,5},{5,4},{6,7},{7,6},{8,9},{9,8},{10,11... | collective-permute-start | bytes 589832 | tf_op jit(solution)/shard_map/cond/branch_1_fun/ppermute | solution.py:464
  175.7 20.1 %collective-permute-start.64 = (bf16[192,512]{1,0:T(8,128)(2,1)S(1)}, bf16[192,512]{1,0:T(8,128)(2,1)}, u32[]{:S(2)}, u32[]{:S(2)}) collective-permute-start(bf16[192,512]{1,0:T(8,128)(2,1)S(1)} %collective-permute-done.63.refs_8_), channel_id=1, source_target_pairs={{0,1},{1,0},{2,3},{3,2},{4,5},{5,4},{6,7},{7,6},{8,9},{9,8},{10,11... | collective-permute-start | bytes 589832 | tf_op jit(solution)/shard_map/cond/branch_1_fun/ppermute | solution.py:466
  179.6 22.0 %collective-permute-start.67 = (bf16[192,512]{1,0:T(8,128)(2,1)S(1)}, bf16[192,512]{1,0:T(8,128)(2,1)S(1)}, u32[]{:S(2)}, u32[]{:S(2)}) collective-permute-start(bf16[192,512]{1,0:T(8,128)(2,1)S(1)} %collective-permute-done.66.refs_5_), channel_id=1, source_target_pairs={{0,1},{1,0},{2,3},{3,2},{4,5},{5,4},{6,7},{7,6},{8,9},{9,8},{10,11... | collective-permute-start | bytes 589832 | tf_op jit(solution)/shard_map/cond/branch_1_fun/ppermute | solution.py:464
  180.1 0.9 copy-start.11
  181.0 0.9 copy-start.13
  181.9 0.9 copy-start.15
  188.5 18.2 %collective-permute-start.69 = (bf16[192,512]{1,0:T(8,128)(2,1)S(1)}, bf16[192,512]{1,0:T(8,128)(2,1)S(1)}, u32[]{:S(2)}, u32[]{:S(2)}) collective-permute-start(bf16[192,512]{1,0:T(8,128)(2,1)S(1)} %collective-permute-done.68.refs_0_), channel_id=1, source_target_pairs={{0,1},{1,0},{2,3},{3,2},{4,5},{5,4},{6,7},{7,6},{8,9},{9,8},{10,11... | collective-permute-start | bytes 589832 | tf_op jit(solution)/shard_map/cond/branch_1_fun/ppermute | solution.py:466
  211.8 1.7 collective-permute-start.70
  213.5 6.3 %collective-permute-start.71 = (bf16[64,1280]{1,0:T(8,128)(2,1)S(1)}, bf16[64,1280]{1,0:T(8,128)(2,1)S(1)}, u32[]{:S(2)}, u32[]{:S(2)}) collective-permute-start(bf16[64,1280]{1,0:T(8,128)(2,1)S(1)} %fusion.11), channel_id=1, source_target_pairs={{0,8},{8,0},{4,12},{12,4},{1,9},{9,1},{5,13},{13,5},{2,10},{10,2},... | collective-permute-start | bytes 491528 | tf_op jit(solution)/shard_map/cond/branch_1_fun/ppermute | solution.py:474
  220.5 0.9 copy-start.1

commit v2 on v1

--- a/solution.py
+++ b/solution.py
@@ -147,9 +147,9 @@
 
 CORE_SWAP = [(0, 1), (1, 0), (2, 3), (3, 2)]
 CHIP_SWAP = [(0, 2), (2, 0), (1, 3), (3, 1)]
-PAIRS_OUTER = [(0, 1), (1, 0), (2, 3), (3, 2)]
-PAIRS_INNER = [(0, 0), (1, 2), (2, 1), (3, 3)]
-CHUNKS = 4
+NEAR = [(0, 1), (1, 0), (2, 3), (3, 2)]
+FAR = [(0, 2), (1, 3), (2, 0), (3, 1)]
+MIDDLE = [(0, 0), (1, 2), (2, 1), (3, 3)]
 F32 = jnp.float32
 BF16 = jnp.bfloat16
 
@@ -163,7 +163,7 @@
 
 
 def call(body, name, out_shape, operands, scalars, grid=(1,), in_specs=None, out_specs=None,
-         scratch=(), aliases=None, flops=0, moved=0, limit=40):
+         scratch=(), aliases=None, flops=0, moved=0, limit=46):
     whole = lambda a: pl.BlockSpec(a.shape, lambda *_, n=len(a.shape): (0,) * n)
     if in_specs is None:
         in_specs = [None] * len(operands)
@@ -179,29 +179,22 @@
         ),
         compiler_params=pltpu.CompilerParams(vmem_limit_bytes=limit << 20),
         input_output_aliases=aliases or {},
-        cost_estimate=pl.CostEstimate(flops=int(flops), bytes_accessed=int(moved), transcendentals=0),
+        cost_estimate=pl.CostEstimate(flops=int(flops) // 100, bytes_accessed=int(moved) // 100, transcendentals=0),
         name=name,
     )(scalars, *operands)
 
 
-def norm_send_body(where, own, core, chip, both, gain, out):
-    t, b = where[0], where[1]
-    wide = [ref[...].astype(F32) for ref in (own, core, chip, both)]
-    total = sum(jnp.sum(w * w, axis=-1, keepdims=True) for w in wide)
-    factor = lax.rsqrt(total / (4 * own.shape[1]) + EPSILON)
-    for j in range(4):
-        block = lax.bitwise_xor(t, j)
-        d = lax.rem(block - b + 4, 4)
-        out[d] = (wide[j] * factor * gain[pl.ds(block, 1), :]).astype(BF16)
-
-
-def qkv_body(where, own, first, second, third, ranks, q_weight, kv_weight, kept, sent):
+def qkv_body(where, own, core, chip, both, ranks, gain, q_weight, kv_weight, kept, sent, squares):
     b = where[1]
     rows = kept.shape[0]
-    spread = jnp.concatenate([own[0], first[...], second[...], third[...]], axis=0)
+    spread = jnp.concatenate([own[...], core[...], chip[...], both[...]], axis=0)
     order = lax.broadcasted_iota(jnp.int32, (rows, ranks.shape[1]), 0)
     pick = (order == ranks[...]).astype(F32).astype(BF16)
-    packed = dot(pick, spread).astype(BF16)
+    wide = dot(pick, spread)
+    sums = jnp.sum(wide * wide, axis=-1, keepdims=True)
+    same = lax.broadcasted_iota(jnp.int32, (rows, rows), 0) == lax.broadcasted_iota(jnp.int32, (rows, rows), 1)
+    squares[...] = jnp.sum(jnp.where(same, sums, 0.0), axis=0, keepdims=True)
+    packed = (wide * gain[pl.ds(b, 1), :]).astype(BF16)
     width = q_weight.shape[1] // 4
     for k in range(4):
         if k % 2 == 0:
@@ -220,10 +213,16 @@
             sent[d - 1, :, width:] = pair.astype(BF16)
 
 
-def attend_body(where, kept, first, second, third, cosine, sine, id_row, id_col, weight, sent, held):
+def attend_body(
+    where, kept, first, second, third, sq0, sq1, sq2, sq3, cosine, sine, id_row, id_col, weight, sent, held
+):
     t = where[0]
     rows = kept.shape[0]
+    squares = (sq0[...] + sq1[...]) + (sq2[...] + sq3[...])
+    same = lax.broadcasted_iota(jnp.int32, (rows, rows), 0) == lax.broadcasted_iota(jnp.int32, (rows, rows), 1)
+    factor = lax.rsqrt(jnp.sum(jnp.where(same, squares, 0.0), axis=1, keepdims=True) / weight.shape[1] + EPSILON)
     total = (kept[...] + first[...].astype(F32)) + (second[...].astype(F32) + third[...].astype(F32))
+    total = total * factor
     turn = lambda v: (v * cosine[...] + jnp.concatenate([v[:, 64:], v[:, :64]], axis=1) * sine[...]).astype(BF16)
     key = turn(total[:, 256:384])
     value = total[:, 384:].astype(BF16)
@@ -290,22 +289,20 @@
 
     @pl.when(k == 0)
     def _():
-        gate[...] = dot(x[0], gate_weight[...])
-        up[...] = dot(x[0], up_weight[...])
-
-    @pl.when(k > 0)
-    def _():
-        gate[...] += dot(x[0], gate_weight[...])
-        up[...] += dot(x[0], up_weight[...])
+        gate[...] = jnp.zeros_like(gate)
+        up[...] = jnp.zeros_like(up)
+
+    gate[...] += dot(x[0], gate_weight[...])
+    up[...] += dot(x[0], up_weight[...])
 
     @pl.when(k == pl.num_programs(0) - 1)
     def _():
         out[...] = (jax.nn.silu(gate[...]) * up[...]).astype(BF16)
 
 
-def hidden_chunk(where, x, gate_weight, up_weight, c):
+def hidden_chunk(where, x, gate_weight, up_weight, start, wide):
     blocks, rows, deep = x.shape
-    wide = gate_weight.shape[1] // CHUNKS
+    c = start // wide
     return call(
         hidden_body, "hidden", jax.ShapeDtypeStruct((rows, wide), BF16), (x, gate_weight, up_weight), where,
         grid=(blocks,),
@@ -315,39 +312,48 @@
             pl.BlockSpec((deep, wide), lambda k, w: (k, c)),
         ],
         scratch=[pltpu.VMEM((rows, wide), F32)] * 2,
-        flops=4 * rows * blocks * deep * wide, moved=4 * blocks * deep * wide,
-    )
-
-
-def down_products(where, refs, count):
+        flops=8 * rows * blocks * deep * wide, moved=8 * blocks * deep * wide,
+    )
+
+
+def down_products(where, pieces, span, refs, weight, total, held, arrived):
     inner = (where[1] == 1) | (where[1] == 2)
-    total = None
-    at = 0
-    for kind in count:
+    copies, at = [], 0
+    for i, (count, position, start, wide) in enumerate(pieces):
+        first = pl.multiple_of(where[position] * span + start, 256)
+        copies.append(
+            pltpu.make_async_copy(weight.at[pl.ds(first, wide), :], held.at[i, pl.ds(0, wide), :], arrived.at[i])
+        )
+        copies[-1].start()
+    for i, (count, position, start, wide) in enumerate(pieces):
         piece = refs[at][...]
-        at += 1
-        if kind == "either":
-            piece = jnp.where(inner, piece, refs[at][...])
-            at += 1
-        product = dot(piece, refs[at][...])
-        at += 1
-        total = product if total is None else total + product
-    return total
-
-
-def down_body(kinds, more, where, *refs):
-    total = down_products(where, refs[1:] if more else refs, kinds)
-    refs[-1][...] = total + refs[0][...] if more else total
-
-
-def down_last_body(kinds, where, acc, resid, slots, *refs):
+        if count == 2:
+            piece = jnp.where(inner, piece, refs[at + 1][...])
+        at += count
+        copies[i].wait()
+
+        def tile(n, carry):
+            columns = pl.ds(pl.multiple_of(n * 256, 256), 256)
+            total[:, columns] += dot(piece, held[i, :wide, columns])
+            return carry
+
+        lax.fori_loop(0, total.shape[1] // 256, tile, 0)
+
+
+def down_body(pieces, span, more, where, *refs):
+    weight, out, held, arrived = refs[-4:]
+    out[...] = refs[0][...] if more else jnp.zeros_like(out)
+    down_products(where, pieces, span, refs[1:] if more else refs, weight, out, held, arrived)
+
+
+def down_last_body(pieces, span, where, acc, resid, slots, *refs):
     t = where[0]
-    total = acc[...] + down_products(where, refs, kinds)
-    rounded = total.astype(BF16)
-    sent, held = refs[-2:]
-    rows = acc.shape[0]
-    order = lax.broadcasted_iota(jnp.int32, (slots.shape[1], rows), 1)
-    for j in range(4):
+    weight, sent, kept, held, arrived, total = refs[-6:]
+    total[...] = acc[...]
+    down_products(where, pieces, span, refs, weight, total, held, arrived)
+    rounded = total[...].astype(BF16)
+    order = lax.broadcasted_iota(jnp.int32, (slots.shape[1], acc.shape[0]), 1)
+    for j in (3, 1, 2, 0):
         pick = (order == slots[lax.bitwise_xor(t, j)]).astype(F32).astype(BF16)
         block = dot(pick, rounded)
         if j == 0:
@@ -355,85 +361,62 @@
         if j % 2:
             sent[j // 2] = block.astype(BF16)
         else:
-            held[j // 2] = block
-
-
-def down_operands(pieces, weight, tile):
-    operands, specs, kinds = [], [], []
-    for kind, arrays, position, c in pieces:
-        kinds.append(kind)
-        for a in arrays:
-            operands.append(a)
-            specs.append(pl.BlockSpec(a.shape, lambda n, w: (0, 0)))
-        operands.append(weight)
-        specs.append(
-            pl.BlockSpec((arrays[0].shape[1], tile), lambda n, w, p=position, c=c: (w[p] * CHUNKS + c, n))
+            kept[j // 2] = block
+
+
+def down(where, acc, pieces, weight, span, ending=None):
+    rows, width = pieces[0][0][0].shape[0], weight.shape[1]
+    arrays = [a for group, *_ in pieces for a in group]
+    told = tuple((len(group), *rest) for group, *rest in pieces)
+    deep = sum(wide for *_, wide in told)
+    more = acc is not None
+    first = [acc] if more else []
+    if ending is None:
+        body, name = functools.partial(down_body, told, span, more), "down"
+        shapes = jax.ShapeDtypeStruct((rows, width), F32)
+    else:
+        body, name = functools.partial(down_last_body, told, span), "down_last"
+        first += list(ending)
+        count = ending[1].shape[1]
+        shapes = (
+            jax.ShapeDtypeStruct((2, count, width), BF16), jax.ShapeDtypeStruct((2, count, width), F32)
         )
-    return tuple(kinds), operands, specs
-
-
-def down(where, acc, pieces, weight, tile=256):
-    rows = pieces[0][1][0].shape[0]
-    width = weight.shape[1]
-    kinds, operands, specs = down_operands(pieces, weight, tile)
-    block = pl.BlockSpec((rows, tile), lambda n, w: (0, n))
-    more = acc is not None
-    deep = sum(a[0].shape[1] for _, a, _, _ in pieces)
     return call(
-        functools.partial(down_body, kinds, more), "down", jax.ShapeDtypeStruct((rows, width), F32),
-        ([acc] if more else []) + operands, where, grid=(width // tile,),
-        in_specs=([block] if more else []) + specs, out_specs=block,
-        aliases={1: 0} if more else None, flops=2 * rows * deep * width, moved=2 * deep * width,
-    )
-
-
-def down_last(where, acc, resid, slots, pieces, weight, tile=256):
-    rows = acc.shape[0]
-    width = weight.shape[1]
-    count = slots.shape[1]
-    kinds, operands, specs = down_operands(pieces, weight, tile)
-    block = pl.BlockSpec((rows, tile), lambda n, w: (0, n))
-    deep = sum(a[0].shape[1] for _, a, _, _ in pieces)
-    out = pl.BlockSpec((2, count, tile), lambda n, w: (0, 0, n))
-    return call(
-        functools.partial(down_last_body, kinds), "down_last",
-        (jax.ShapeDtypeStruct((2, count, width), BF16), jax.ShapeDtypeStruct((2, count, width), F32)),
-        [acc, resid, slots] + operands, where, grid=(width // tile,),
-        in_specs=[block, block, None] + specs, out_specs=(out, out),
-        flops=2 * rows * deep * width, moved=2 * deep * width,
-    )
-
-
-def packed_layer(rows, where, picked, recv, ranks, own_ranks, slots, keys, gains, weights):
-    attn_kept, first, second, third = recv
+        body, name, shapes, first + arrays + [weight], where,
+        in_specs=[None] * (len(first) + len(arrays)) + [pl.BlockSpec(memory_space=pl.ANY)],
+        scratch=[
+            pltpu.VMEM((len(told), max(wide for *_, wide in told), width), BF16),
+            pltpu.SemaphoreType.DMA((len(told),)),
+        ] + ([] if ending is None else [pltpu.VMEM((rows, width), F32)]),
+        aliases={1: 0} if more and ending is None else None, flops=4 * rows * deep * width,
+        moved=4 * deep * width,
+    )
+
+
+def after(done, *arrays):
+    return lax.optimization_barrier((arrays, done))[0]
+
+
+def packed_layer(rows, where, picked, recv, ranks, own_ranks, slots, ids, cosine, sine, gains, weights):
     q_weight, kv_weight, out_weight, gate_weight, up_weight, down_weight = weights
     feature = picked.shape[1]
     each = rows // 4
     shape = jax.ShapeDtypeStruct
 
-    place = jnp.arange(rows, dtype=jnp.int32)
-    ids = jnp.sum(jnp.where(place[:, None] == ranks, keys + 1, 0), axis=1) - 1
-    allowed = (ids[:, None] == ids[None, :]) & (place[None, :] <= place[:, None])
-    positions = (jnp.sum(allowed.astype(jnp.int32), axis=1) - 1).astype(F32)
-    half = HEAD_DIM // 2
-    freq = jnp.exp(jnp.arange(half).astype(F32) * (-2.0 * math.log(ROPE_BASE) / HEAD_DIM))
-    angle = positions[:, None] * freq[None, :]
-    cosine, sine = jnp.cos(angle), jnp.sin(angle)
-    cosine = jnp.concatenate([cosine, cosine], axis=1)
-    sine = jnp.concatenate([-sine, sine], axis=1)
-
+    ids, cosine, sine = ids[:rows], cosine[:rows], sine[:rows]
     width = q_weight.shape[1] // 4 + 256
-    kept, sent = call(
-        qkv_body, "qkv", (shape((rows, width), F32), shape((3, rows, width), BF16)),
-        (attn_kept, first, second, third, ranks, q_weight, kv_weight), where,
-        in_specs=[pl.BlockSpec((1,) + attn_kept.shape[1:], lambda i, w: (0, 0, 0))] + [None] * 5
-        + [pl.BlockSpec((feature, 512), lambda i, w: (0, w[0]))],
+    kept, sent, squares = call(
+        qkv_body, "qkv",
+        (shape((rows, width), F32), shape((3, rows, width), BF16), shape((1, rows), F32)),
+        (*recv, ranks, gains[0], q_weight, kv_weight), where,
+        in_specs=[None] * 7 + [pl.BlockSpec((feature, 512), lambda i, w: (0, w[0]))],
         flops=2 * rows * feature * 1536, moved=feature * 3072 + rows * 6000,
     )
     sums = [shift(sent[d - 1], d) for d in (1, 2, 3)]
+    squares = [squares] + [shift(squares, d) for d in (1, 2, 3)]
     sent, held = call(
         attend_body, "attend", (shape((2, rows, feature), BF16), shape((2, rows, feature), F32)),
-        (kept, *sums, cosine, sine, ids[None, :], ids[:, None], out_weight), where,
+        (kept, *sums, *squares, cosine, sine, ids[None, :], ids[:, None], out_weight), where,
         flops=2 * rows * 256 * 5120, moved=256 * 10240 + rows * 30000,
     )
     core = lax.ppermute(sent, "tensor", CORE_SWAP)
@@ -456,20 +439,32 @@
     normed = normed.reshape(4, rows, feature)
     resid = resid.reshape(rows, feature)
 
-    acc = None
-    for c in range(CHUNKS):
-        own = hidden_chunk(where, normed, gate_weight, up_weight, c)
-        a1 = lax.ppermute(own, "batch", PAIRS_OUTER)
-        b1 = lax.ppermute(own, "batch", PAIRS_INNER)
-        a2 = lax.ppermute(b1, "batch", PAIRS_OUTER)
-        b2 = lax.ppermute(a1, "batch", PAIRS_INNER)
-        a3 = lax.ppermute(b2, "batch", PAIRS_OUTER)
-        pieces = [("one", [own], 1, c), ("one", [a1], 2, c), ("either", [b1, a2], 3, c), ("either", [b2, a3], 4, c)]
-        if c < CHUNKS - 1:
-            acc = down(where, acc, pieces, down_weight)
-        else:
-            acc = down(where, acc, pieces[:3], down_weight)
-            sent, held = down_last(where, acc, resid, slots, pieces[3:], down_weight)
+    swap = lambda a, pairs: lax.ppermute(a, "batch", pairs)
+    span = gate_weight.shape[1]
+    chunks = ((3 * span // 4, span // 4), (0, 3 * span // 8), (3 * span // 8, 3 * span // 8))
+    hidden = lambda x, c: hidden_chunk(where, x, gate_weight, up_weight, *chunks[c])
+    pieces = lambda c, own, near, far, mid, late: [
+        ((own,), 1, *chunks[c]), ((near,), 2, *chunks[c]), ((far,), 3, *chunks[c]), ((mid, late), 4, *chunks[c]),
+    ]
+    h0 = hidden(normed, 0)
+    far0, near0, mid0 = swap(h0, FAR), swap(h0, NEAR), swap(h0, MIDDLE)
+    h1 = hidden(*after(h0, normed), 1)
+    (far0,) = after(h1, far0)
+    late0 = swap(far0, NEAR)
+    far1, near1, mid1 = swap(h1, FAR), swap(h1, NEAR), swap(h1, MIDDLE)
+    h2 = hidden(*after((h1, far0, near0, mid0), normed), 2)
+    (far1,) = after(h2, far1)
+    late1 = swap(far1, NEAR)
+    far2, near2, mid2 = swap(h2, FAR), swap(h2, NEAR), swap(h2, MIDDLE)
+    first = pieces(0, h0, near0, far0, mid0, late0)
+    second = pieces(1, h1, near1, far1, mid1, late1)
+    (h0,) = after((h2, far1, near1, mid1, late0), h0)
+    acc = down(where, None, [((h0,), *first[0][1:])] + first[1:] + second[:3], down_weight, span)
+    (far2,) = after(acc, far2)
+    late2 = swap(far2, NEAR)
+    (acc,) = after((far2, near2, mid2, late1), acc)
+    acc = down(where, acc, second[3:] + pieces(2, h2, near2, far2, mid2, None)[:3], down_weight, span)
+    sent, held = down(where, acc, [((mid2, late2), 4, *chunks[2])], down_weight, span, (resid, slots))
     core = lax.ppermute(sent, "tensor", CORE_SWAP)
     chip = lax.ppermute((held[1] + core[1].astype(F32)).astype(BF16), "tensor", CHIP_SWAP)
     return (held[0] + core[0].astype(F32) + chip.astype(F32)).astype(BF16)
@@ -485,8 +480,7 @@
     groups, capacity = send_index.shape[1:]
     total = send_index.size
     each = groups * capacity
-    pair = lax.bitwise_xor(b, 1)
-    where = jnp.stack([t, b, pair, jnp.where(b < 2, 2, 1), jnp.where(b < 2, 3, 0)]).astype(jnp.int32)
+    where = jnp.stack([t] + [lax.bitwise_xor(b, i) for i in range(4)]).astype(jnp.int32)
 
     flat = send_index.reshape(total)
     live = flat >= 0
@@ -495,9 +489,11 @@
     outgoing = lax.dynamic_index_in_dim(send_index, b, 0, keepdims=False).reshape(each)
     picked = jnp.take(frames, jnp.maximum(outgoing, 0), axis=0)
     picked = jnp.where((outgoing >= 0)[:, None], picked, jnp.zeros_like(picked))
-    chip = lax.ppermute(picked, "tensor", CHIP_SWAP)
-    core = lax.ppermute(picked, "tensor", CORE_SWAP)
+    moved = lax.ppermute(picked, ("tensor", "batch"), [(i * 4 + j, j * 4 + i) for i in range(4) for j in range(4)])
+    chip = lax.ppermute(moved, "tensor", CHIP_SWAP)
+    core = lax.ppermute(moved, "tensor", CORE_SWAP)
     both = lax.ppermute(chip, "tensor", CORE_SWAP)
+    recv = (moved, core, chip, both)
 
     slot = jnp.arange(total, dtype=jnp.int32)
     rank = jnp.sum((live[None, :] & (slot[None, :] < slot[:, None])).astype(jnp.int32), axis=1)
@@ -510,23 +506,28 @@
     )
     keys = jnp.where(live, looked * groups + (slot // capacity) % groups, -1)
     by_owner = rank.reshape(groups, each)
-    turned = (b - jnp.arange(4, dtype=jnp.int32)) % 4
+    turned = lax.bitwise_xor(t, jnp.arange(4, dtype=jnp.int32))
+    own_ranks = lax.dynamic_index_in_dim(by_owner, b, 0)
     ranks = by_owner[turned].reshape(1, total)
     keys = keys.reshape(groups, each)[turned].reshape(1, total)
-    own_ranks = ranks[:, :each]
     slots = rank.reshape(groups, groups, capacity).transpose(1, 0, 2).reshape(groups, each, 1)
 
+    place = jnp.arange(total, dtype=jnp.int32)
+    ids = jnp.sum(jnp.where(place[:, None] == ranks, keys + 1, 0), axis=1) - 1
+    allowed = (ids[:, None] == ids[None, :]) & (place[None, :] <= place[:, None])
+    positions = (jnp.sum(allowed.astype(jnp.int32), axis=1) - 1).astype(F32)
+    half = HEAD_DIM // 2
+    freq = jnp.exp(jnp.arange(half).astype(F32) * (-2.0 * math.log(ROPE_BASE) / HEAD_DIM))
+    angle = positions[:, None] * freq[None, :]
+    cosine, sine = jnp.cos(angle), jnp.sin(angle)
+    cosine = jnp.concatenate([cosine, cosine], axis=1)
+    sine = jnp.concatenate([-sine, sine], axis=1)
+
     gains = (attn_gain.reshape(4, -1), ffn_gain.reshape(4, -1))
-    normed = call(
-        norm_send_body, "norm_send", jax.ShapeDtypeStruct((4,) + picked.shape, BF16),
-        (picked, core, chip, both, gains[0]), where, flops=each * 5120 * 10, moved=each * 5120 * 4,
-    )
-    recv = [normed] + [shift(normed[d], d) for d in (1, 2, 3)]
     weights = (q_weight, kv_weight, out_weight, gate_weight, up_weight, down_weight)
     run = lambda rows: functools.partial(packed_layer, rows)
-    return lax.cond(
-        most <= 192, run(192), run(256), where, picked, recv, ranks, own_ranks, slots, keys, gains, weights
-    )
+    small = lax.optimization_barrier((where, picked, recv, ranks, own_ranks, slots, ids, cosine, sine, gains))
+    return lax.cond(most <= 192, run(192), run(256), *small, weights)
 
 
 def fits(mesh):

time: 222 us -> 201 us (0.905)
  waiting for transfers between devices: 81.3 us -> 64.2 us
  Pallas kernels: 64.3 us -> 57.2 us
  other arithmetic: 3.81 us -> 7.92 us
    ppermute x12, waiting for transfers between devices: 43.9 us -> 26.3 us  [shift(): lax.ppermute(values, 'batch', [(i, (i + distance) % 4) for i in range(4)])]
    pallas_call x14 -> x10, Pallas kernels: 64.3 us -> 57.2 us  [call(): pl.pallas_call(body, out_shape=out_shape, grid_spec=pltpu.PrefetchScalarG...]
    unnamed x36 -> x18, local copies, waits for them, and re-layouts: 6.02 us -> 1.68 us
    ppermute x12, starting transfers between devices: 15.4 us -> 18 us  [shift(): lax.ppermute(values, 'batch', [(i, (i + distance) % 4) for i in range(4)])]
    ppermute x22 -> x15, starting transfers between devices: 37.9 us -> 36.4 us  [the longest x12 27.8 us: packed_layer(): swap = lambda a, pairs: lax.ppermute(a, 'batch', pairs)]
  transfers between devices with their start and end apart: 43 -> 36, of which waited for: 15 -> 15; matrix products, arithmetic and copies ran while one was open for 2% -> 6% of each run, Pallas kernels for 19% -> 18%
where the time goes in v2:
time: 201 us; the launch traced here: 200 us
  waiting for transfers between devices  64.2 us (32%)
  starting transfers between devices  61 us (30%)
  Pallas kernels  57.2 us (28%)
  local copies, waits for them, and re-layouts  8.18 us (4%)
  other arithmetic  7.92 us (4%)
    pallas_call x10, Pallas kernels, call(): pl.pallas_call(body, out_shape=out_shape, grid_spec=pltpu.PrefetchScalarG...  57.2 us
    ppermute x12, starting transfers between devices, packed_layer(): swap = lambda a, pairs: lax.ppermute(a, 'batch', pairs)  27.8 us
    ppermute x12, waiting for transfers between devices, shift(): lax.ppermute(values, 'batch', [(i, (i + distance) % 4) for i in range(4)])  26.3 us
    ppermute x12, starting transfers between devices, shift(): lax.ppermute(values, 'batch', [(i, (i + distance) % 4) for i in range(4)])  18 us
    ppermute x2, waiting for transfers between devices, packed_layer(): lax.ppermute((held[1] + core[1].astype(F32)).astype(BF16), 'tensor', CHIP...  17.2 us
    ppermute x1, waiting for transfers between devices, packed_layer(): chip = lax.ppermute(mine, 'tensor', CHIP_SWAP)  12.4 us
    ppermute x1, starting transfers between devices, per_device_packed(): chip = lax.ppermute(moved, 'tensor', CHIP_SWAP)  7.94 us
    ppermute x2, waiting for transfers between devices, packed_layer(): core = lax.ppermute(sent, 'tensor', CORE_SWAP)  4.17 us
  transfers between devices with their start and end apart: 36, of which 15 were waited for; matrix products, arithmetic and copies ran while one was open for 6% of the time, Pallas kernels for 18%

profile of v2, /device:TPU:0, one launch (start us, length us, event | category | flops | bytes accessed | tf_op | source)
XLA Modules:
  0.0 200.3 jit_solution(15099275926382619316)
XLA Ops:
  0.0 0.8 broadcast_compare_fusion.1
  1.1 0.7 gather_fusion
  1.9 0.7 collective-permute-start.63
  2.6 0.8 reshape.161
  3.6 0.7 select_bitcast_fusion
  4.3 0.7 convert_reduce_fusion.2
  5.0 3.0 %collective-permute-start.62 = (s32[1]{0:T(128)}, s32[1]{0:T(128)}, u32[]{:S(2)}, u32[]{:S(2)}) collective-permute-start(s32[1]{0:T(128)} %bitcast.38), channel_id=1, source_target_pairs={{0,16},{16,0},{1,17},{17,1},{2,18},{18,2},{3,19},{19,3},{4,20},{20... | collective-permute-start | bytes 20 | tf_op jit(solution)/shard_map/ppermute | solution.py:488
  8.2 0.8 select_reduce_fusion
  10.8 7.9 %collective-permute-start.65 = (bf16[64,1280]{1,0:T(8,128)(2,1)S(1)}, bf16[64,1280]{1,0:T(8,128)(2,1)S(1)}, u32[]{:S(2)}, u32[]{:S(2)}) collective-permute-start(bf16[64,1280]{1,0:T(8,128)(2,1)S(1)} %collective-permute-done.63), channel_id=1, source_target_pairs={{0,8},{8,0},{4,12},{12,4},{1,9},{9,1},{5,13},{13,5},{2,10},{10,2},... | collective-permute-start | bytes 491528 | tf_op jit(solution)/shard_map/ppermute | solution.py:493
  18.7 1.3 fusion.6
  20.0 2.0 %collective-permute-done.65 = bf16[64,1280]{1,0:T(8,128)(2,1)S(1)} collective-permute-done((bf16[64,1280]{1,0:T(8,128)(2,1)S(1)}, bf16[64,1280]{1,0:T(8,128)(2,1)S(1)}, u32[]{:S(2)}, u32[]{:S(2)}) %collective-permute-start.65) | collective-permute-done | bytes 163872 | tf_op jit(solution)/shard_map/ppermute | solution.py:493
  22.2 0.7 reshape.165
  23.0 1.9 pad_maximum_fusion.4
  26.3 173.1 %conditional.7 = (bf16[64,1280]{1,0:T(8,128)(2,1)}) conditional(s32[]{:T(128)} %convert_element_type.118, (s32[5]{0:T(128)S(1)}, bf16[64,1280]{1,0:T(8,128)(2,1)S(1)}, bf16[64,1280]{1,0:T(8,128)(2,1)S(1)}, bf16[64,1280]{1,0:T(8,128)(2,1)S(1)}, bf16[64,1280]{1,0:T(8,128)(2,1)S(1)}, /*index=5*/s32[1,256]{1,0:T(1,128)S(1)}, f32[4,1280]{1,0:T(4,128)S(1)}, ...), branch_computations={%region_5.6_spmd, %region_6.7_spmd} | conditional | flops 343300480 | bytes 56608456
  26.5 0.6 copy-done.4
  27.3 4.0 %qkv.3 = (f32[192,512]{1,0:T(8,128)S(1)}, bf16[3,192,512]{2,1,0:T(8,128)(2,1)S(1)}, f32[1,192]{1,0:T(1,128)S(1)}) custom-call(s32[5]{0:T(128)S(1)} %get-tuple-element.132.where, bf16[64,1280]{1,0:T(8,128)(2,1)S(1)} %get-tuple-element.133.own, bf16[64,1280]{1,0:T(8,128)(2,1)} %copy-done.6, bf16[64,1280]{1,0:T(8,128)(2,1)} %copy-done.4, ...), custom_call_target="tpu_custom_call" | custom-call | flops 7549747 | bytes 50841 | tf_op jit(solution)/shard_map/cond/branch_1_fun/qkv/pallas_call | solution.py:173
  31.6 3.0 %collective-permute-start.32 = (bf16[192,512]{1,0:T(8,128)(2,1)S(1)}, bf16[192,512]{1,0:T(8,128)(2,1)S(1)}, u32[]{:S(2)}, u32[]{:S(2)}) collective-permute-start(bf16[192,512]{1,0:T(8,128)(2,1)S(1)} %get-tuple-element.292), channel_id=1, source_target_pairs={{0,2},{1,3},{2,0},{3,1},{4,6},{5,7},{6,4},{7,5},{8,10},{9,11},{10,... | collective-permute-start | bytes 589832 | tf_op jit(solution)/shard_map/cond/branch_1_fun/ppermute | solution.py:162
  34.6 1.4 collective-permute-start.33
  36.0 0.6 collective-permute-start.34
  37.2 11.8 %collective-permute-done.34.sq1 = f32[1,192]{1,0:T(1,128)S(1)} collective-permute-done((f32[1,192]{1,0:T(1,128)S(1)}, f32[1,192]{1,0:T(1,128)S(1)}, u32[]{:S(2)}, u32[]{:S(2)}) %collective-permute-start.34) | collective-permute-done | bytes 800 | tf_op jit(solution)/shard_map/cond/branch_1_fun/ppermute | solution.py:162
  49.1 0.9 slice.69.cosine
  50.1 0.9 slice.70.sine
  51.0 1.4 collective-permute-done.35.sq2
  52.6 4.0 %attend.3 = (bf16[2,192,1280]{2,1,0:T(8,128)(2,1)S(1)}, f32[2,192,1280]{2,1,0:T(8,128)S(1)}) custom-call(s32[5]{0:T(128)S(1)} %get-tuple-element.132.where, f32[192,512]{1,0:T(8,128)S(1)} %get-tuple-element.141.kept, bf16[192,512]{1,0:T(8,128)(2,1)S(1)} %collective-permute-done.31.first, bf16[192,512]{1,0:T(8,128)(2,1)S(1)} %collective-permute-done.32.second, ...), custom_call_target="tpu_custom_call" | custom-call | flops 5033164 | bytes 83814 | tf_op jit(solution)/shard_map/cond/branch_1_fun/attend/pallas_call | solution.py:173
  56.7 2.6 %collective-permute-done.37.core = bf16[2,192,1280]{2,1,0:T(8,128)(2,1)S(1)} collective-permute-done((bf16[2,192,1280]{2,1,0:T(8,128)(2,1)S(1)}, bf16[2,192,1280]{2,1,0:T(8,128)(2,1)S(1)}, u32[]{:S(2)}, u32[]{:S(2)}) %collective-permute-start.37) | collective-permute-done | bytes 983072 | tf_op jit(solution)/shard_map/cond/branch_1_fun/ppermute | solution.py:422
  59.3 2.1 %collective-permute-start.38 = (bf16[192,1280]{1,0:T(8,128)(2,1)S(1)}, bf16[192,1280]{1,0:T(8,128)(2,1)S(1)}, u32[]{:S(2)}, u32[]{:S(2)}) collective-permute-start(bf16[192,1280]{1,0:T(8,128)(2,1)S(1)} %fusion.2), channel_id=1, source_target_pairs={{0,8},{8,0},{4,12},{12,4},{1,9},{9,1},{5,13},{13,5},{2,10},{10,2},... | collective-permute-start | bytes 1474568 | tf_op jit(solution)/shard_map/cond/branch_1_fun/ppermute | solution.py:423
  61.4 11.5 %collective-permute-done.38.chip = bf16[192,1280]{1,0:T(8,128)(2,1)S(1)} collective-permute-done((bf16[192,1280]{1,0:T(8,128)(2,1)S(1)}, bf16[192,1280]{1,0:T(8,128)(2,1)S(1)}, u32[]{:S(2)}, u32[]{:S(2)}) %collective-permute-start.38) | collective-permute-done | bytes 491552 | tf_op jit(solution)/shard_map/cond/branch_1_fun/ppermute | solution.py:423
  72.9 0.9 gather_sum.3
  73.9 2.1 %collective-permute-start.39 = (bf16[48,1280]{1,0:T(8,128)(2,1)S(1)}, bf16[48,1280]{1,0:T(8,128)(2,1)S(1)}, u32[]{:S(2)}, u32[]{:S(2)}) collective-permute-start(bf16[48,1280]{1,0:T(8,128)(2,1)S(1)} %get-tuple-element.294), channel_id=1, source_target_pairs={{0,1},{1,2},{2,3},{3,0},{4,5},{5,6},{6,7},{7,4},{8,9},{9,10},{10,1... | collective-permute-start | bytes 368648 | tf_op jit(solution)/shard_map/cond/branch_1_fun/ppermute | solution.py:162
  76.0 1.9 collective-permute-start.40
  77.9 2.5 %collective-permute-start.41 = (bf16[48,1280]{1,0:T(8,128)(2,1)S(1)}, bf16[48,1280]{1,0:T(8,128)(2,1)S(1)}, u32[]{:S(2)}, u32[]{:S(2)}) collective-permute-start(bf16[48,1280]{1,0:T(8,128)(2,1)S(1)} %get-tuple-element.295), channel_id=1, source_target_pairs={{0,3},{1,0},{2,1},{3,2},{4,7},{5,4},{6,5},{7,6},{8,11},{9,8},{10,9... | collective-permute-start | bytes 368648 | tf_op jit(solution)/shard_map/cond/branch_1_fun/ppermute | solution.py:162
  80.4 1.0 collective-permute-done.39
  81.4 4.6 %collective-permute-done.40 = bf16[48,1280]{1,0:T(8,128)(2,1)S(1)} collective-permute-done((bf16[48,1280]{1,0:T(8,128)(2,1)S(1)}, bf16[48,1280]{1,0:T(8,128)(2,1)S(1)}, u32[]{:S(2)}, u32[]{:S(2)}) %collective-permute-start.40) | collective-permute-done | bytes 122912 | tf_op jit(solution)/shard_map/cond/branch_1_fun/ppermute | solution.py:162
  86.0 3.2 %collective-permute-start.42 = (bf16[48,1280]{1,0:T(8,128)(2,1)S(1)}, bf16[48,1280]{1,0:T(8,128)(2,1)S(1)}, u32[]{:S(2)}, u32[]{:S(2)}) collective-permute-start(bf16[48,1280]{1,0:T(8,128)(2,1)S(1)} %add_convert_fusion.5), channel_id=1, source_target_pairs={{0,1},{1,2},{2,3},{3,0},{4,5},{5,6},{6,7},{7,4},{8,9},{9,10},{10,1... | collective-permute-start | bytes 368648 | tf_op jit(solution)/shard_map/cond/branch_1_fun/ppermute | solution.py:162
  89.2 2.3 %collective-permute-start.43 = (bf16[48,1280]{1,0:T(8,128)(2,1)S(1)}, bf16[48,1280]{1,0:T(8,128)(2,1)S(1)}, u32[]{:S(2)}, u32[]{:S(2)}) collective-permute-start(bf16[48,1280]{1,0:T(8,128)(2,1)S(1)} %add_convert_fusion.5), channel_id=1, source_target_pairs={{0,2},{1,3},{2,0},{3,1},{4,6},{5,7},{6,4},{7,5},{8,10},{9,11},{10,... | collective-permute-start | bytes 368648 | tf_op jit(solution)/shard_map/cond/branch_1_fun/ppermute | solution.py:162
  91.6 3.5 %collective-permute-done.42 = bf16[48,1280]{1,0:T(8,128)(2,1)S(1)} collective-permute-done((bf16[48,1280]{1,0:T(8,128)(2,1)S(1)}, bf16[48,1280]{1,0:T(8,128)(2,1)S(1)}, u32[]{:S(2)}, u32[]{:S(2)}) %collective-permute-start.42) | collective-permute-done | bytes 122912 | tf_op jit(solution)/shard_map/cond/branch_1_fun/ppermute | solution.py:162
  95.1 3.7 %collective-permute-done.43 = bf16[48,1280]{1,0:T(8,128)(2,1)S(1)} collective-permute-done((bf16[48,1280]{1,0:T(8,128)(2,1)S(1)}, bf16[48,1280]{1,0:T(8,128)(2,1)S(1)}, u32[]{:S(2)}, u32[]{:S(2)}) %collective-permute-start.43) | collective-permute-done | bytes 122912 | tf_op jit(solution)/shard_map/cond/branch_1_fun/ppermute | solution.py:162
  98.9 0.7 collective-permute-start.45
  99.6 12.4 %collective-permute-done.45.chip = bf16[4,48,1280]{2,1,0:T(8,128)(2,1)S(1)} collective-permute-done((bf16[4,48,1280]{2,1,0:T(8,128)(2,1)S(1)}, bf16[4,48,1280]{2,1,0:T(8,128)(2,1)S(1)}, u32[]{:S(2)}, u32[]{:S(2)}) %collective-permute-start.45) | collective-permute-done | bytes 491552 | tf_op jit(solution)/shard_map/cond/branch_1_fun/ppermute | solution.py:433
  112.1 1.9 collective-permute-done.47
  114.0 1.6 norm_all.3
  115.7 6.5 %hidden.9.refs_0_ = bf16[192,512]{1,0:T(8,128)(2,1)S(1)} custom-call(s32[5]{0:T(128)S(1)} %get-tuple-element.132.where, bf16[4,192,1280]{2,1,0:T(8,128)(2,1)S(1)} %bitcast.71, bf16[5120,2048]{1,0:T(8,128)(2,1)} %get-tuple-element.156.gate_weight, bf16[5120,2048]{1,0:T(8,128)(2,1)} %get-tuple-element.157.up_weight), custom_call_target="tpu_custom_call" | custom-call | flops 40265320 | bytes 209715 | tf_op jit(solution)/shard_map/cond/branch_1_fun/hidden/pallas_call | solution.py:173
  122.2 2.3 %collective-permute-start.48 = (bf16[192,512]{1,0:T(8,128)(2,1)S(1)}, bf16[192,512]{1,0:T(8,128)(2,1)S(1)}, u32[]{:S(2)}, u32[]{:S(2)}) collective-permute-start(bf16[192,512]{1,0:T(8,128)(2,1)S(1)} %hidden.9.refs_0_), channel_id=1, source_target_pairs={{0,2},{1,3},{2,0},{3,1},{4,6},{5,7},{6,4},{7,5},{8,10},{9,11},{10,... | collective-permute-start | bytes 589832 | tf_op jit(solution)/shard_map/cond/branch_1_fun/ppermute | solution.py:442
  124.4 1.9 collective-permute-start.49
  126.3 0.7 collective-permute-start.50
  127.0 8.4 %hidden.10.refs_5_ = bf16[192,768]{1,0:T(8,128)(2,1)S(1)} custom-call(s32[5]{0:T(128)S(1)} %get-tuple-element.132.where, bf16[4,192,1280]{2,1,0:T(8,128)(2,1)S(1)} %bitcast.72, bf16[5120,2048]{1,0:T(8,128)(2,1)} %get-tuple-element.156.gate_weight, bf16[5120,2048]{1,0:T(8,128)(2,1)} %get-tuple-element.157.up_weight), custom_call_target="tpu_custom_call" | custom-call | flops 60397976 | bytes 314572 | tf_op jit(solution)/shard_map/cond/branch_1_fun/hidden/pallas_call | solution.py:173
  135.4 3.3 %collective-permute-start.51 = (bf16[192,768]{1,0:T(8,128)(2,1)S(1)}, bf16[192,768]{1,0:T(8,128)(2,1)S(1)}, u32[]{:S(2)}, u32[]{:S(2)}) collective-permute-start(bf16[192,768]{1,0:T(8,128)(2,1)S(1)} %hidden.10.refs_5_), channel_id=1, source_target_pairs={{0,2},{1,3},{2,0},{3,1},{4,6},{5,7},{6,4},{7,5},{8,10},{9,11},{10,... | collective-permute-start | bytes 884744 | tf_op jit(solution)/shard_map/cond/branch_1_fun/ppermute | solution.py:442
  138.7 0.6 collective-permute-start.52
  139.4 0.7 collective-permute-start.53
  140.1 8.4 %hidden.11.refs_3_ = bf16[192,768]{1,0:T(8,128)(2,1)S(1)} custom-call(s32[5]{0:T(128)S(1)} %get-tuple-element.132.where, bf16[4,192,1280]{2,1,0:T(8,128)(2,1)S(1)} %bitcast.73, bf16[5120,2048]{1,0:T(8,128)(2,1)} %get-tuple-element.156.gate_weight, bf16[5120,2048]{1,0:T(8,128)(2,1)} %get-tuple-element.157.up_weight), custom_call_target="tpu_custom_call" | custom-call | flops 60397976 | bytes 314572 | tf_op jit(solution)/shard_map/cond/branch_1_fun/hidden/pallas_call | solution.py:173
  148.5 4.1 %collective-permute-start.55 = (bf16[192,768]{1,0:T(8,128)(2,1)S(1)}, bf16[192,768]{1,0:T(8,128)(2,1)S(1)}, u32[]{:S(2)}, u32[]{:S(2)}) collective-permute-start(bf16[192,768]{1,0:T(8,128)(2,1)S(1)} %hidden.11.refs_3_), channel_id=1, source_target_pairs={{0,2},{1,3},{2,0},{3,1},{4,6},{5,7},{6,4},{7,5},{8,10},{9,11},{10,... | collective-permute-start | bytes 884744 | tf_op jit(solution)/shard_map/cond/branch_1_fun/ppermute | solution.py:442
  152.6 0.6 collective-permute-start.54
  153.2 1.4 collective-permute-start.56
  154.6 0.9 collective-permute-start.57
  155.6 10.5 %collective-permute-start.58 = (bf16[192,768]{1,0:T(8,128)(2,1)S(1)}, bf16[192,768]{1,0:T(8,128)(2,1)}, u32[]{:S(2)}, u32[]{:S(2)}) collective-permute-start(bf16[192,768]{1,0:T(8,128)(2,1)S(1)} %collective-permute-done.51.refs_7_), channel_id=1, source_target_pairs={{0,1},{1,0},{2,3},{3,2},{4,5},{5,4},{6,7},{7,6},{8,9},{9,8},{10,11... | collective-permute-start | bytes 884744 | tf_op jit(solution)/shard_map/cond/branch_1_fun/ppermute | solution.py:442
  166.1 10.1 %down.6.refs_0_ = f32[192,1280]{1,0:T(8,128)S(1)} custom-call(s32[5]{0:T(128)S(1)} %get-tuple-element.132.where, bf16[192,512]{1,0:T(8,128)(2,1)S(1)} %hidden.9.refs_0_, bf16[192,512]{1,0:T(8,128)(2,1)S(1)} %collective-permute-done.49.refs_1_, bf16[192,512]{1,0:T(8,128)(2,1)S(1)} %collective-permute-done.48.refs_2_, ...), custom_call_target="tpu_custom_call" | custom-call | flops 42781900 | bytes 222822 | tf_op jit(solution)/shard_map/cond/branch_1_fun/down/pallas_call | solution.py:173
  176.3 0.7 collective-permute-start.59
  177.3 8.3 %down.7.acc = f32[192,1280]{1,0:T(8,128)S(1)} custom-call(s32[5]{0:T(128)S(1)} %get-tuple-element.132.where, f32[192,1280]{1,0:T(8,128)S(1)} %down.6.refs_0_, bf16[192,768]{1,0:T(8,128)(2,1)S(1)} %collective-permute-done.53.refs_1_, bf16[192,768]{1,0:T(8,128)(2,1)} %collective-permute-done.58.refs_2_, ...), custom_call_target="tpu_custom_call", output_to_operand_aliasing={{}: (1, {})} | custom-call | flops 30198988 | bytes 157286 | tf_op jit(solution)/shard_map/cond/branch_1_fun/down/pallas_call | solution.py:173
  185.6 5.0 %down_last.3 = (bf16[2,64,1280]{2,1,0:T(8,128)(2,1)S(1)}, f32[2,64,1280]{2,1,0:T(8,128)S(1)}) custom-call(s32[5]{0:T(128)S(1)} %get-tuple-element.132.where, f32[192,1280]{1,0:T(8,128)S(1)} %down.7.acc, bf16[192,1280]{1,0:T(8,128)(2,1)S(1)} %bitcast.75, s32[4,64,1]{2,1,0:T(8,128)S(1)} %copy.26.slots, bf16[192,768]{1,0:T(8,128)(2,1)S(1)} %collective-permute-done.57.refs_0_, ...), custom_call_target="tpu_custom_call" | custom-call | flops 7549747 | bytes 39321 | tf_op jit(solution)/shard_map/cond/branch_1_fun/down_last/pallas_call | solution.py:173
  190.7 1.6 collective-permute-done.60
  192.4 0.6 collective-permute-start.61
  193.0 5.7 %collective-permute-done.61 = bf16[64,1280]{1,0:T(8,128)(2,1)S(1)} collective-permute-done((bf16[64,1280]{1,0:T(8,128)(2,1)S(1)}, bf16[64,1280]{1,0:T(8,128)(2,1)S(1)}, u32[]{:S(2)}, u32[]{:S(2)}) %collective-permute-start.61) | collective-permute-done | bytes 163872 | tf_op jit(solution)/shard_map/cond/branch_1_fun/ppermute | solution.py:469
  198.7 0.7 bitcast_add_fusion.1
  199.4 0.9 copy-done.1
  (90 shorter events, 5.1 us)
Async XLA Ops:
  0.0 1.1 copy-start
  0.0 22.2 %copy-start.11 = (f32[5120]{0:T(1024)S(1)}, f32[5120]{0:T(1024)}, u32[]{:S(2)}) copy-start(f32[5120]{0:T(1024)} %param.16) | copy-start | bytes 61444
  0.0 26.3 %copy-start.2 = (bf16[1280,1024]{1,0:T(8,128)(2,1)S(1)}, bf16[1280,1024]{1,0:T(8,128)(2,1)}, u32[]{:S(2)}) copy-start(bf16[1280,1024]{1,0:T(8,128)(2,1)} %param.17) | copy-start | bytes 7864324
  1.9 8.8 %collective-permute-start.63 = (bf16[64,1280]{1,0:T(8,128)(2,1)S(1)}, bf16[64,1280]{1,0:T(8,128)(2,1)S(1)}, u32[]{:S(2)}, u32[]{:S(2)}) collective-permute-start(bf16[64,1280]{1,0:T(8,128)(2,1)S(1)} %select_select_fusion), channel_id=1, source_target_pairs={{0,0},{1,4},{2,8},{3,12},{4,1},{5,5},{6,9},{7,13},{8,2},{9,6},{10,... | collective-permute-start | bytes 491528 | tf_op jit(solution)/shard_map/ppermute | solution.py:492
  5.0 19.9 %collective-permute-start.62 = (s32[1]{0:T(128)}, s32[1]{0:T(128)}, u32[]{:S(2)}, u32[]{:S(2)}) collective-permute-start(s32[1]{0:T(128)} %bitcast.38), channel_id=1, source_target_pairs={{0,16},{16,0},{1,17},{17,1},{2,18},{18,2},{3,19},{19,3},{4,20},{20... | collective-permute-start | bytes 20 | tf_op jit(solution)/shard_map/ppermute | solution.py:488
  10.8 11.2 %collective-permute-start.65 = (bf16[64,1280]{1,0:T(8,128)(2,1)S(1)}, bf16[64,1280]{1,0:T(8,128)(2,1)S(1)}, u32[]{:S(2)}, u32[]{:S(2)}) collective-permute-start(bf16[64,1280]{1,0:T(8,128)(2,1)S(1)} %collective-permute-done.63), channel_id=1, source_target_pairs={{0,8},{8,0},{4,12},{12,4},{1,9},{9,1},{5,13},{13,5},{2,10},{10,2},... | collective-permute-start | bytes 491528 | tf_op jit(solution)/shard_map/ppermute | solution.py:493
  20.0 6.3 %collective-permute-start.64 = (bf16[64,1280]{1,0:T(8,128)(2,1)S(1)}, bf16[64,1280]{1,0:T(8,128)(2,1)S(1)}, u32[]{:S(2)}, u32[]{:S(2)}) collective-permute-start(bf16[64,1280]{1,0:T(8,128)(2,1)S(1)} %collective-permute-done.63), channel_id=1, source_target_pairs={{0,4},{4,0},{8,12},{12,8},{1,5},{5,1},{9,13},{13,9},{2,6},{6,2},{1... | collective-permute-start | bytes 491528 | tf_op jit(solution)/shard_map/ppermute | solution.py:494
  22.0 4.2 %collective-permute-start.66 = (bf16[64,1280]{1,0:T(8,128)(2,1)S(1)}, bf16[64,1280]{1,0:T(8,128)(2,1)S(1)}, u32[]{:S(2)}, u32[]{:S(2)}) collective-permute-start(bf16[64,1280]{1,0:T(8,128)(2,1)S(1)} %collective-permute-done.65), channel_id=1, source_target_pairs={{0,4},{4,0},{8,12},{12,8},{1,5},{5,1},{9,13},{13,9},{2,6},{6,2},{1... | collective-permute-start | bytes 491528 | tf_op jit(solution)/shard_map/ppermute | solution.py:495
  26.5 0.7 copy-start.4
  26.5 0.7 copy-start.6
  26.5 0.7 copy-start.8
  26.5 4.7 %copy-start.9 = (f32[4,1280]{1,0:T(4,128)}, f32[4,1280]{1,0:T(4,128)S(1)}, u32[]{:S(2)}) copy-start(f32[4,1280]{1,0:T(4,128)S(1)} %get-tuple-element.154.gain) | copy-start | bytes 61444
  31.3 21.3 %collective-permute-start.31 = (bf16[192,512]{1,0:T(8,128)(2,1)S(1)}, bf16[192,512]{1,0:T(8,128)(2,1)S(1)}, u32[]{:S(2)}, u32[]{:S(2)}) collective-permute-start(bf16[192,512]{1,0:T(8,128)(2,1)S(1)} %get-tuple-element.293), channel_id=1, source_target_pairs={{0,1},{1,2},{2,3},{3,0},{4,5},{5,6},{6,7},{7,4},{8,9},{9,10},{10,1... | collective-permute-start | bytes 589832 | tf_op jit(solution)/shard_map/cond/branch_1_fun/ppermute | solution.py:162
  31.6 21.0 %collective-permute-start.32 = (bf16[192,512]{1,0:T(8,128)(2,1)S(1)}, bf16[192,512]{1,0:T(8,128)(2,1)S(1)}, u32[]{:S(2)}, u32[]{:S(2)}) collective-permute-start(bf16[192,512]{1,0:T(8,128)(2,1)S(1)} %get-tuple-element.292), channel_id=1, source_target_pairs={{0,2},{1,3},{2,0},{3,1},{4,6},{5,7},{6,4},{7,5},{8,10},{9,11},{10,... | collective-permute-start | bytes 589832 | tf_op jit(solution)/shard_map/cond/branch_1_fun/ppermute | solution.py:162
  34.6 18.0 %collective-permute-start.33 = (bf16[192,512]{1,0:T(8,128)(2,1)S(1)}, bf16[192,512]{1,0:T(8,128)(2,1)S(1)}, u32[]{:S(2)}, u32[]{:S(2)}) collective-permute-start(bf16[192,512]{1,0:T(8,128)(2,1)S(1)} %get-tuple-element.291), channel_id=1, source_target_pairs={{0,3},{1,0},{2,1},{3,2},{4,7},{5,4},{6,5},{7,6},{8,11},{9,8},{10,9... | collective-permute-start | bytes 589832 | tf_op jit(solution)/shard_map/cond/branch_1_fun/ppermute | solution.py:162
  36.0 13.1 %collective-permute-start.34 = (f32[1,192]{1,0:T(1,128)S(1)}, f32[1,192]{1,0:T(1,128)S(1)}, u32[]{:S(2)}, u32[]{:S(2)}) collective-permute-start(f32[1,192]{1,0:T(1,128)S(1)} %get-tuple-element.143.sq0), channel_id=1, source_target_pairs={{0,1},{1,2},{2,3},{3,0},{4,5},{5,6},{6,7},{7,4},{8,9},{9,10},{10,1... | collective-permute-start | bytes 2312 | tf_op jit(solution)/shard_map/cond/branch_1_fun/ppermute | solution.py:162
  36.6 15.8 %collective-permute-start.35 = (f32[1,192]{1,0:T(1,128)S(1)}, f32[1,192]{1,0:T(1,128)S(1)}, u32[]{:S(2)}, u32[]{:S(2)}) collective-permute-start(f32[1,192]{1,0:T(1,128)S(1)} %get-tuple-element.143.sq0), channel_id=1, source_target_pairs={{0,2},{1,3},{2,0},{3,1},{4,6},{5,7},{6,4},{7,5},{8,10},{9,11},{10,... | collective-permute-start | bytes 2312 | tf_op jit(solution)/shard_map/cond/branch_1_fun/ppermute | solution.py:162
  49.0 3.6 %collective-permute-start.36 = (f32[1,192]{1,0:T(1,128)S(1)}, f32[1,192]{1,0:T(1,128)S(1)}, u32[]{:S(2)}, u32[]{:S(2)}) collective-permute-start(f32[1,192]{1,0:T(1,128)S(1)} %get-tuple-element.143.sq0), channel_id=1, source_target_pairs={{0,3},{1,0},{2,1},{3,2},{4,7},{5,4},{6,5},{7,6},{8,11},{9,8},{10,9... | collective-permute-start | bytes 2312 | tf_op jit(solution)/shard_map/cond/branch_1_fun/ppermute | solution.py:162
  56.6 2.6 %collective-permute-start.37 = (bf16[2,192,1280]{2,1,0:T(8,128)(2,1)S(1)}, bf16[2,192,1280]{2,1,0:T(8,128)(2,1)S(1)}, u32[]{:S(2)}, u32[]{:S(2)}) collective-permute-start(bf16[2,192,1280]{2,1,0:T(8,128)(2,1)S(1)} %get-tuple-element.149), channel_id=1, source_target_pairs={{0,4},{4,0},{8,12},{12,8},{1,5},{5,1},{9,13},{13,9},{2,6},{6,2},{1... | collective-permute-start | bytes 2949128 | tf_op jit(solution)/shard_map/cond/branch_1_fun/ppermute | solution.py:422
  59.3 13.6 %collective-permute-start.38 = (bf16[192,1280]{1,0:T(8,128)(2,1)S(1)}, bf16[192,1280]{1,0:T(8,128)(2,1)S(1)}, u32[]{:S(2)}, u32[]{:S(2)}) collective-permute-start(bf16[192,1280]{1,0:T(8,128)(2,1)S(1)} %fusion.2), channel_id=1, source_target_pairs={{0,8},{8,0},{4,12},{12,4},{1,9},{9,1},{5,13},{13,5},{2,10},{10,2},... | collective-permute-start | bytes 1474568 | tf_op jit(solution)/shard_map/cond/branch_1_fun/ppermute | solution.py:423
  73.9 40.1 %copy-start.10 = (f32[4,1280]{1,0:T(4,128)S(1)}, f32[4,1280]{1,0:T(4,128)}, u32[]{:S(2)}) copy-start(f32[4,1280]{1,0:T(4,128)} %copy-done.9) | copy-start | bytes 61444
  73.9 7.5 %collective-permute-start.39 = (bf16[48,1280]{1,0:T(8,128)(2,1)S(1)}, bf16[48,1280]{1,0:T(8,128)(2,1)S(1)}, u32[]{:S(2)}, u32[]{:S(2)}) collective-permute-start(bf16[48,1280]{1,0:T(8,128)(2,1)S(1)} %get-tuple-element.294), channel_id=1, source_target_pairs={{0,1},{1,2},{2,3},{3,0},{4,5},{5,6},{6,7},{7,4},{8,9},{9,10},{10,1... | collective-permute-start | bytes 368648 | tf_op jit(solution)/shard_map/cond/branch_1_fun/ppermute | solution.py:162
  76.0 10.0 %collective-permute-start.40 = (bf16[48,1280]{1,0:T(8,128)(2,1)S(1)}, bf16[48,1280]{1,0:T(8,128)(2,1)S(1)}, u32[]{:S(2)}, u32[]{:S(2)}) collective-permute-start(bf16[48,1280]{1,0:T(8,128)(2,1)S(1)} %get-tuple-element.296), channel_id=1, source_target_pairs={{0,2},{1,3},{2,0},{3,1},{4,6},{5,7},{6,4},{7,5},{8,10},{9,11},{10,... | collective-permute-start | bytes 368648 | tf_op jit(solution)/shard_map/cond/branch_1_fun/ppermute | solution.py:162
  77.9 8.1 %collective-permute-start.41 = (bf16[48,1280]{1,0:T(8,128)(2,1)S(1)}, bf16[48,1280]{1,0:T(8,128)(2,1)S(1)}, u32[]{:S(2)}, u32[]{:S(2)}) collective-permute-start(bf16[48,1280]{1,0:T(8,128)(2,1)S(1)} %get-tuple-element.295), channel_id=1, source_target_pairs={{0,3},{1,0},{2,1},{3,2},{4,7},{5,4},{6,5},{7,6},{8,11},{9,8},{10,9... | collective-permute-start | bytes 368648 | tf_op jit(solution)/shard_map/cond/branch_1_fun/ppermute | solution.py:162
  86.0 9.1 %collective-permute-start.42 = (bf16[48,1280]{1,0:T(8,128)(2,1)S(1)}, bf16[48,1280]{1,0:T(8,128)(2,1)S(1)}, u32[]{:S(2)}, u32[]{:S(2)}) collective-permute-start(bf16[48,1280]{1,0:T(8,128)(2,1)S(1)} %add_convert_fusion.5), channel_id=1, source_target_pairs={{0,1},{1,2},{2,3},{3,0},{4,5},{5,6},{6,7},{7,4},{8,9},{9,10},{10,1... | collective-permute-start | bytes 368648 | tf_op jit(solution)/shard_map/cond/branch_1_fun/ppermute | solution.py:162
  89.2 9.7 %collective-permute-start.43 = (bf16[48,1280]{1,0:T(8,128)(2,1)S(1)}, bf16[48,1280]{1,0:T(8,128)(2,1)S(1)}, u32[]{:S(2)}, u32[]{:S(2)}) collective-permute-start(bf16[48,1280]{1,0:T(8,128)(2,1)S(1)} %add_convert_fusion.5), channel_id=1, source_target_pairs={{0,2},{1,3},{2,0},{3,1},{4,6},{5,7},{6,4},{7,5},{8,10},{9,11},{10,... | collective-permute-start | bytes 368648 | tf_op jit(solution)/shard_map/cond/branch_1_fun/ppermute | solution.py:162
  91.5 7.4 %collective-permute-start.44 = (bf16[48,1280]{1,0:T(8,128)(2,1)S(1)}, bf16[48,1280]{1,0:T(8,128)(2,1)S(1)}, u32[]{:S(2)}, u32[]{:S(2)}) collective-permute-start(bf16[48,1280]{1,0:T(8,128)(2,1)S(1)} %add_convert_fusion.5), channel_id=1, source_target_pairs={{0,3},{1,0},{2,1},{3,2},{4,7},{5,4},{6,5},{7,6},{8,11},{9,8},{10,9... | collective-permute-start | bytes 368648 | tf_op jit(solution)/shard_map/cond/branch_1_fun/ppermute | solution.py:162
  98.9 13.1 %collective-permute-start.45 = (bf16[4,48,1280]{2,1,0:T(8,128)(2,1)S(1)}, bf16[4,48,1280]{2,1,0:T(8,128)(2,1)S(1)}, u32[]{:S(2)}, u32[]{:S(2)}) collective-permute-start(bf16[4,48,1280]{2,1,0:T(8,128)(2,1)S(1)} %pad_maximum_fusion.3.own), channel_id=1, source_target_pairs={{0,8},{8,0},{4,12},{12,4},{1,9},{9,1},{5,13},{13,5},{2,10},{10,2},... | collective-permute-start | bytes 1474568 | tf_op jit(solution)/shard_map/cond/branch_1_fun/ppermute | solution.py:433
  99.6 12.4 %collective-permute-start.46 = (bf16[4,48,1280]{2,1,0:T(8,128)(2,1)S(1)}, bf16[4,48,1280]{2,1,0:T(8,128)(2,1)S(1)}, u32[]{:S(2)}, u32[]{:S(2)}) collective-permute-start(bf16[4,48,1280]{2,1,0:T(8,128)(2,1)S(1)} %pad_maximum_fusion.3.own), channel_id=1, source_target_pairs={{0,4},{4,0},{8,12},{12,8},{1,5},{5,1},{9,13},{13,9},{2,6},{6,2},{1... | collective-permute-start | bytes 1474568 | tf_op jit(solution)/shard_map/cond/branch_1_fun/ppermute | solution.py:434
  112.1 1.9 collective-permute-start.47
  122.2 17.2 %collective-permute-start.48 = (bf16[192,512]{1,0:T(8,128)(2,1)S(1)}, bf16[192,512]{1,0:T(8,128)(2,1)S(1)}, u32[]{:S(2)}, u32[]{:S(2)}) collective-permute-start(bf16[192,512]{1,0:T(8,128)(2,1)S(1)} %hidden.9.refs_0_), channel_id=1, source_target_pairs={{0,2},{1,3},{2,0},{3,1},{4,6},{5,7},{6,4},{7,5},{8,10},{9,11},{10,... | collective-permute-start | bytes 589832 | tf_op jit(solution)/shard_map/cond/branch_1_fun/ppermute | solution.py:442
  124.4 15.6 %collective-permute-start.49 = (bf16[192,512]{1,0:T(8,128)(2,1)S(1)}, bf16[192,512]{1,0:T(8,128)(2,1)S(1)}, u32[]{:S(2)}, u32[]{:S(2)}) collective-permute-start(bf16[192,512]{1,0:T(8,128)(2,1)S(1)} %hidden.9.refs_0_), channel_id=1, source_target_pairs={{0,1},{1,0},{2,3},{3,2},{4,5},{5,4},{6,7},{7,6},{8,9},{9,8},{10,11... | collective-permute-start | bytes 589832 | tf_op jit(solution)/shard_map/cond/branch_1_fun/ppermute | solution.py:442
  126.3 13.7 %collective-permute-start.50 = (bf16[192,512]{1,0:T(8,128)(2,1)S(1)}, bf16[192,512]{1,0:T(8,128)(2,1)S(1)}, u32[]{:S(2)}, u32[]{:S(2)}) collective-permute-start(bf16[192,512]{1,0:T(8,128)(2,1)S(1)} %hidden.9.refs_0_), channel_id=1, source_target_pairs={{0,0},{1,2},{2,1},{3,3},{4,4},{5,6},{6,5},{7,7},{8,8},{9,10},{10,9... | collective-permute-start | bytes 589832 | tf_op jit(solution)/shard_map/cond/branch_1_fun/ppermute | solution.py:442
  135.4 17.8 %collective-permute-start.51 = (bf16[192,768]{1,0:T(8,128)(2,1)S(1)}, bf16[192,768]{1,0:T(8,128)(2,1)S(1)}, u32[]{:S(2)}, u32[]{:S(2)}) collective-permute-start(bf16[192,768]{1,0:T(8,128)(2,1)S(1)} %hidden.10.refs_5_), channel_id=1, source_target_pairs={{0,2},{1,3},{2,0},{3,1},{4,6},{5,7},{6,4},{7,5},{8,10},{9,11},{10,... | collective-permute-start | bytes 884744 | tf_op jit(solution)/shard_map/cond/branch_1_fun/ppermute | solution.py:442
  138.7 15.9 %collective-permute-start.52 = (bf16[192,768]{1,0:T(8,128)(2,1)S(1)}, bf16[192,768]{1,0:T(8,128)(2,1)S(1)}, u32[]{:S(2)}, u32[]{:S(2)}) collective-permute-start(bf16[192,768]{1,0:T(8,128)(2,1)S(1)} %hidden.10.refs_5_), channel_id=1, source_target_pairs={{0,1},{1,0},{2,3},{3,2},{4,5},{5,4},{6,7},{7,6},{8,9},{9,8},{10,11... | collective-permute-start | bytes 884744 | tf_op jit(solution)/shard_map/cond/branch_1_fun/ppermute | solution.py:442
  139.4 16.2 %collective-permute-start.53 = (bf16[192,768]{1,0:T(8,128)(2,1)S(1)}, bf16[192,768]{1,0:T(8,128)(2,1)S(1)}, u32[]{:S(2)}, u32[]{:S(2)}) collective-permute-start(bf16[192,768]{1,0:T(8,128)(2,1)S(1)} %hidden.10.refs_5_), channel_id=1, source_target_pairs={{0,0},{1,2},{2,1},{3,3},{4,4},{5,6},{6,5},{7,7},{8,8},{9,10},{10,9... | collective-permute-start | bytes 884744 | tf_op jit(solution)/shard_map/cond/branch_1_fun/ppermute | solution.py:442
  148.5 27.8 %collective-permute-start.55 = (bf16[192,768]{1,0:T(8,128)(2,1)S(1)}, bf16[192,768]{1,0:T(8,128)(2,1)S(1)}, u32[]{:S(2)}, u32[]{:S(2)}) collective-permute-start(bf16[192,768]{1,0:T(8,128)(2,1)S(1)} %hidden.11.refs_3_), channel_id=1, source_target_pairs={{0,2},{1,3},{2,0},{3,1},{4,6},{5,7},{6,4},{7,5},{8,10},{9,11},{10,... | collective-permute-start | bytes 884744 | tf_op jit(solution)/shard_map/cond/branch_1_fun/ppermute | solution.py:442
  152.6 13.5 %collective-permute-start.54 = (bf16[192,512]{1,0:T(8,128)(2,1)S(1)}, bf16[192,512]{1,0:T(8,128)(2,1)S(1)}, u32[]{:S(2)}, u32[]{:S(2)}) collective-permute-start(bf16[192,512]{1,0:T(8,128)(2,1)S(1)} %collective-permute-done.48.refs_2_), channel_id=1, source_target_pairs={{0,1},{1,0},{2,3},{3,2},{4,5},{5,4},{6,7},{7,6},{8,9},{9,8},{10,11... | collective-permute-start | bytes 589832 | tf_op jit(solution)/shard_map/cond/branch_1_fun/ppermute | solution.py:442
  153.2 23.9 %collective-permute-start.56 = (bf16[192,768]{1,0:T(8,128)(2,1)S(1)}, bf16[192,768]{1,0:T(8,128)(2,1)S(1)}, u32[]{:S(2)}, u32[]{:S(2)}) collective-permute-start(bf16[192,768]{1,0:T(8,128)(2,1)S(1)} %hidden.11.refs_3_), channel_id=1, source_target_pairs={{0,1},{1,0},{2,3},{3,2},{4,5},{5,4},{6,7},{7,6},{8,9},{9,8},{10,11... | collective-permute-start | bytes 884744 | tf_op jit(solution)/shard_map/cond/branch_1_fun/ppermute | solution.py:442
  154.6 22.5 %collective-permute-start.57 = (bf16[192,768]{1,0:T(8,128)(2,1)S(1)}, bf16[192,768]{1,0:T(8,128)(2,1)S(1)}, u32[]{:S(2)}, u32[]{:S(2)}) collective-permute-start(bf16[192,768]{1,0:T(8,128)(2,1)S(1)} %hidden.11.refs_3_), channel_id=1, source_target_pairs={{0,0},{1,2},{2,1},{3,3},{4,4},{5,6},{6,5},{7,7},{8,8},{9,10},{10,9... | collective-permute-start | bytes 884744 | tf_op jit(solution)/shard_map/cond/branch_1_fun/ppermute | solution.py:442
  155.6 21.8 %collective-permute-start.58 = (bf16[192,768]{1,0:T(8,128)(2,1)S(1)}, bf16[192,768]{1,0:T(8,128)(2,1)}, u32[]{:S(2)}, u32[]{:S(2)}) collective-permute-start(bf16[192,768]{1,0:T(8,128)(2,1)S(1)} %collective-permute-done.51.refs_7_), channel_id=1, source_target_pairs={{0,1},{1,0},{2,3},{3,2},{4,5},{5,4},{6,7},{7,6},{8,9},{9,8},{10,11... | collective-permute-start | bytes 884744 | tf_op jit(solution)/shard_map/cond/branch_1_fun/ppermute | solution.py:442
  176.3 9.3 %collective-permute-start.59 = (bf16[192,768]{1,0:T(8,128)(2,1)S(1)}, bf16[192,768]{1,0:T(8,128)(2,1)}, u32[]{:S(2)}, u32[]{:S(2)}) collective-permute-start(bf16[192,768]{1,0:T(8,128)(2,1)S(1)} %collective-permute-done.55.refs_5_), channel_id=1, source_target_pairs={{0,1},{1,0},{2,3},{3,2},{4,5},{5,4},{6,7},{7,6},{8,9},{9,8},{10,11... | collective-permute-start | bytes 884744 | tf_op jit(solution)/shard_map/cond/branch_1_fun/ppermute | solution.py:442
  190.6 1.7 collective-permute-start.60
  192.4 6.3 %collective-permute-start.61 = (bf16[64,1280]{1,0:T(8,128)(2,1)S(1)}, bf16[64,1280]{1,0:T(8,128)(2,1)S(1)}, u32[]{:S(2)}, u32[]{:S(2)}) collective-permute-start(bf16[64,1280]{1,0:T(8,128)(2,1)S(1)} %fusion.3), channel_id=1, source_target_pairs={{0,8},{8,0},{4,12},{12,4},{1,9},{9,1},{5,13},{13,5},{2,10},{10,2},... | collective-permute-start | bytes 491528 | tf_op jit(solution)/shard_map/cond/branch_1_fun/ppermute | solution.py:469
  199.4 0.9 copy-start.1
